TPU v7x, 512 devices: a whole 4x4x16 slice. The times are simulated.
512 devices in a mesh: section: 16 (over y, x), expert: 32 (over z, core).
Axes of the slice: x: 4, y: 4, z: 16, core: 2. Of those that a mesh axis runs over, the one named last changes fastest.
Arguments:
- in_flight: bfloat16 [16, 2, 1024, 1024], P('section', None, 'expert'), may hold values from -6 to 6
- arriving: bfloat16 [1, 2, 1024, 1024], P(None, None, 'expert'), may hold values from -6 to 6
- norm_gain: float32 [16, 1024], P('section'), may hold values from 0.1 to 1.9
- gate_up: bfloat16 [16, 32, 1024, 1536], P('section', 'expert'), may hold values from -0.1875 to 0.1875
- w_down: bfloat16 [16, 32, 768, 1024], P('section', 'expert'), may hold values from -0.21875 to 0.21875
- expert_ids: int32 [2, 16, 2, 1024, 8], P(None, 'section', None, 'expert'), may hold values from 0 to 31, all different within a row; in each aligned block of 32 rows (0 to 31, 32 to 63, ..., all dimensions but the last counted through in order) at most 16 rows name the same one
- route_weights: float32 [2, 16, 2, 1024, 8], P(None, 'section', None, 'expert'), may hold values from 0.05 to 1
Outputs:
- section_outputs: bfloat16 [2, 16, 2, 1024, 1024], P(None, 'section', None, 'expert')
Inputs may be any that keep to these rules, and one draw needn't show every extreme that they name: `expert_ids`: each token names 8 different experts. In each micro-batch of each step and section, the tokens of one aligned block of 32 (the rows of one device) name one expert at most 16 times.
All inputs are finite; a program needn't handle non-finite values.
Results may differ from a plain program's by a relative error of at most 0.007.
Values may be sent and summed in bfloat16 or wider, within the bound.
A program may use at most 64 MiB of HBM per device.

v0:
```python
import jax
import jax.numpy as jnp
from jax import lax
from jax.sharding import PartitionSpec as P


def shifted(value, axis, by):
    size = lax.axis_size(axis)
    pairs = [(i, i + by) for i in range(size) if 0 <= i + by < size]
    return lax.ppermute(value, axis, pairs)


def normalize(inflow, gain_row):
    widened = inflow.astype(jnp.float32)
    inverse_rms = lax.rsqrt(jnp.mean(widened * widened, axis=-1, keepdims=True) + 1e-06)
    return (widened * inverse_rms * gain_row).astype(jnp.bfloat16)


def run_experts(buffer, gate_up, w_down):
    hidden_count = w_down.shape[2]
    row_block = buffer[:, :, 0].reshape(-1, buffer.shape[-1])
    projected = jnp.dot(row_block, gate_up[0, 0], preferred_element_type=jnp.float32)
    hidden = (jax.nn.silu(projected[:, :hidden_count]) * projected[:, hidden_count:]).astype(
        jnp.bfloat16
    )
    result = jnp.dot(hidden, w_down[0, 0], preferred_element_type=jnp.float32).astype(jnp.bfloat16)
    outputs = [result.reshape(buffer.shape[:2] + buffer.shape[3:])]
    return jnp.stack(outputs, axis=2)


def local(in_flight, arriving, norm_gain, gate_up, w_down, expert_ids, route_weights):
    owners = lax.axis_size("expert")
    local_count = gate_up.shape[1]
    experts_all = owners * local_count
    micro_count = in_flight.shape[1]
    tokens_mb = in_flight.shape[2]
    features = in_flight.shape[3]
    top_count = expert_ids.shape[-1]
    capacity = max(tokens_mb // 2, tokens_mb * top_count // experts_all)
    is_first = lax.axis_index("section") == 0
    gain_row = norm_gain[0][None, None, :]
    outputs = []
    inflow = in_flight[0]
    for step_number in range(expert_ids.shape[0]):
        if step_number > 0:
            incoming = shifted(outputs[-1], "section", 1)
            inflow = jnp.where(is_first, arriving[step_number - 1], incoming)
        normed = normalize(inflow, gain_row)
        step_ids = expert_ids[step_number, 0]
        flat_ids = step_ids.reshape(micro_count, tokens_mb * top_count)
        onehot = (
            flat_ids[:, :, None] == jnp.arange(experts_all, dtype=jnp.int32)[None, None, :]
        ).astype(jnp.int32)
        earlier = jnp.cumsum(onehot, axis=1) - onehot
        slot_of = jnp.sum(earlier * onehot, axis=-1)
        target = (flat_ids * capacity + slot_of).reshape(micro_count, tokens_mb, top_count)
        row_index = jnp.arange(experts_all * capacity, dtype=jnp.int32)
        picker = jnp.sum(
            (target[:, None, :, :] == row_index[None, :, None, None]).astype(jnp.int32), axis=3
        ).astype(jnp.bfloat16)
        outgoing = jnp.einsum(
            "mri,mid->mrd", picker, normed, preferred_element_type=jnp.float32
        ).astype(jnp.bfloat16)
        outgoing = outgoing.reshape(micro_count, experts_all, capacity, features)
        received = lax.all_to_all(outgoing, "expert", split_axis=1, concat_axis=1, tiled=True)
        count = received.shape[0]
        buffer = received.reshape(count, owners, local_count, capacity, features)
        served = run_experts(buffer, gate_up, w_down).reshape(
            count, experts_all, capacity, features
        )
        returned = lax.all_to_all(served, "expert", split_axis=1, concat_axis=1, tiled=True)
        picked = jnp.take_along_axis(
            returned.reshape(micro_count, experts_all * capacity, features),
            target.reshape(micro_count, tokens_mb * top_count, 1),
            axis=1,
        )
        weights_now = route_weights[step_number, 0][..., None]
        branch = jnp.sum(
            picked.reshape(micro_count, tokens_mb, top_count, features).astype(jnp.float32)
            * weights_now,
            axis=2,
        )
        outputs.append((inflow.astype(jnp.float32) + branch).astype(jnp.bfloat16))
    return jnp.stack(outputs)[:, None]


def solution(mesh):
    return jax.shard_map(
        local,
        mesh=mesh,
        in_specs=(
            P("section", None, "expert", None),
            P(None, None, "expert", None),
            P("section", None),
            P("section", "expert", None, None),
            P("section", "expert", None, None),
            P(None, "section", None, "expert", None),
            P(None, "section", None, "expert", None),
        ),
        out_specs=P(None, "section", None, "expert", None),
        check_vma=False,
    )
```

profile of v0, /device:TPU:25, one launch (start us, length us, event | category | flops | bytes accessed | tf_op | source)
XLA Modules:
  0.0 496.3 jit_solution(17864462322573729082)
XLA Ops:
  0.0 0.9 fusion.43
  1.1 1.0 fusion.15
  2.2 1.2 reduce-window.14
  4.2 1.7 convolution_convert_fusion.1
  6.2 116.4 %all_to_all.20 = bf16[2,32,16,1024]{3,2,0,1:T(8,128)(2,1)S(1)} all-to-all(bf16[2,32,16,1024]{3,2,0,1:T(8,128)(2,1)S(1)} %copy.46), channel_id=1, replica_groups=mesh['section'=16,'expert'=32] {'expert'}, dimensions={1} | all-to-all | bytes 4194304 | tf_op jit(solution)/shard_map/all_to_all | solution.py:65
  122.9 3.4 fusion.4
  126.4 1.8 convolution_convert_fusion.3
  128.2 1.5 copy.48
  129.7 5.0 %all-to-all-start.1 = ((bf16[2,32,16,1024]{3,2,0,1:T(8,128)(2,1)}), bf16[2,32,16,1024]{3,2,0,1:T(8,128)(2,1)}, u32[]{:S(2)}, u32[]{:S(2)}) async-start(bf16[2,32,16,1024]{3,2,0,1:T(8,128)(2,1)} %copy.48), calls=%async_computation.1 | async-start | bytes 4194304 | tf_op jit(solution)/shard_map/all_to_all | solution.py:71
  135.8 1.2 reduce-window.16
  138.6 95.2 %all-to-all-done.1 = bf16[2,32,16,1024]{3,2,0,1:T(8,128)(2,1)} async-done(((bf16[2,32,16,1024]{3,2,0,1:T(8,128)(2,1)}), bf16[2,32,16,1024]{3,2,0,1:T(8,128)(2,1)}, u32[]{:S(2)}, u32[]{:S(2)}) %all-to-all-start.1) | async-done | bytes 2097184 | tf_op jit(solution)/shard_map/all_to_all | solution.py:71
  233.8 3.2 copy.49
  237.0 10.5 %gather_fusion = bf16[512,1024]{1,0:T(8,128)(2,1)} fusion(bf16[2,512,1024]{2,1,0:T(8,128)(2,1)} %bitcast.141, s32[512]{0:T(512)S(1)} %bitcast.143), kind=kCustom, calls=%fused_computation.clone | custom fusion | bytes 2101248 | tf_op jit(solution)/shard_map/jit(take_along_axis)/gather | solution.py:72
  247.6 2.1 fusion.7
  250.4 3.1 collective-permute-start
  253.5 1.4 bitcast_add_fusion
  254.9 1.1 convert_reduce_fusion
  256.1 2.5 collective-permute-done
  258.5 1.1 fusion.20
  259.6 0.8 convolution_convert_fusion
  260.7 107.3 %all_to_all.21 = bf16[2,32,16,1024]{3,2,0,1:T(8,128)(2,1)S(1)} all-to-all(bf16[2,32,16,1024]{3,2,0,1:T(8,128)(2,1)S(1)} %copy.53), channel_id=1, replica_groups=mesh['section'=16,'expert'=32] {'expert'}, dimensions={1} | all-to-all | bytes 4194304 | tf_op jit(solution)/shard_map/all_to_all | solution.py:65
  368.4 3.4 fusion.2
  371.8 1.8 convolution_convert_fusion.2
  373.6 1.5 copy.55
  375.1 5.4 %all-to-all-start.3 = ((bf16[2,32,16,1024]{3,2,0,1:T(8,128)(2,1)}), bf16[2,32,16,1024]{3,2,0,1:T(8,128)(2,1)}, u32[]{:S(2)}, u32[]{:S(2)}) async-start(bf16[2,32,16,1024]{3,2,0,1:T(8,128)(2,1)} %copy.55), calls=%async_computation.3 | async-start | bytes 4194304 | tf_op jit(solution)/shard_map/all_to_all | solution.py:71
  381.2 1.4 broadcast_multiply_fusion
  382.6 0.8 mul.141
  384.1 95.5 %all-to-all-done.3 = bf16[2,32,16,1024]{3,2,0,1:T(8,128)(2,1)} async-done(((bf16[2,32,16,1024]{3,2,0,1:T(8,128)(2,1)}), bf16[2,32,16,1024]{3,2,0,1:T(8,128)(2,1)}, u32[]{:S(2)}, u32[]{:S(2)}) %all-to-all-start.3) | async-done | bytes 2097184 | tf_op jit(solution)/shard_map/all_to_all | solution.py:71
  479.7 3.2 copy.56
  482.9 10.6 %gather_fusion.1 = bf16[512,1024]{1,0:T(8,128)(2,1)} fusion(bf16[2,512,1024]{2,1,0:T(8,128)(2,1)} %bitcast.142, s32[512]{0:T(512)S(1)} %bitcast.144), kind=kCustom, calls=%fused_computation.1.clone | custom fusion | bytes 2101248 | tf_op jit(solution)/shard_map/jit(take_along_axis)/gather | solution.py:72
  493.4 2.1 fusion.6
  495.6 0.7 maximum_bitcast_fusion
  (62 shorter events, 7.2 us)
Async XLA Ops:
  0.0 122.9 %copy-start = (bf16[1,1,1024,1536]{3,2,1,0:T(8,128)(2,1)S(1)}, bf16[1,1,1024,1536]{3,2,1,0:T(8,128)(2,1)}, u32[]{:S(2)}) copy-start(bf16[1,1,1024,1536]{3,2,1,0:T(8,128)(2,1)} %param.12) | copy-start | bytes 9437188
  122.9 3.4 copy-start.9
  129.7 5.4 %copy-start.8 = (f32[2,1,2,32,8]{3,4,2,1,0:T(8,128)S(1)}, f32[2,1,2,32,8]{3,4,2,1,0:T(8,128)}, u32[]{:S(2)}) copy-start(f32[2,1,2,32,8]{3,4,2,1,0:T(8,128)} %param.15) | copy-start | bytes 12292
  129.7 104.2 %all-to-all-start.1 = ((bf16[2,32,16,1024]{3,2,0,1:T(8,128)(2,1)}), bf16[2,32,16,1024]{3,2,0,1:T(8,128)(2,1)}, u32[]{:S(2)}, u32[]{:S(2)}) async-start(bf16[2,32,16,1024]{3,2,0,1:T(8,128)(2,1)} %copy.48), calls=%async_computation.1 | async-start | bytes 4194304 | tf_op jit(solution)/shard_map/all_to_all | solution.py:71
  134.7 1.0 copy-start.4
  237.0 12.7 %copy-start.1 = (bf16[1,2,32,1024]{3,2,1,0:T(8,128)(2,1)S(1)}, bf16[1,2,32,1024]{3,2,1,0:T(8,128)(2,1)}, u32[]{:S(2)}) copy-start(bf16[1,2,32,1024]{3,2,1,0:T(8,128)(2,1)} %param.9) | copy-start | bytes 393220
  247.6 12.1 %copy-start.7 = (f32[1,1024]{1,0:T(1,128)S(1)}, f32[1,1024]{1,0:T(1,128)}, u32[]{:S(2)}) copy-start(f32[1,1024]{1,0:T(1,128)} %param.11) | copy-start | bytes 12292
  250.4 8.1 %collective-permute-start = (bf16[2,32,1024]{2,1,0:T(8,128)(2,1)}, bf16[2,32,1024]{2,1,0:T(8,128)(2,1)}, u32[]{:S(2)}, u32[]{:S(2)}) collective-permute-start(bf16[2,32,1024]{2,1,0:T(8,128)(2,1)} %fusion.18), channel_id=1, source_target_pairs={{0,32},{32,64},{64,96},{96,128},{128,160},{160,192},{192,224},{224... | collective-permute-start | bytes 393224 | tf_op jit(solution)/shard_map/ppermute | solution.py:10
  259.6 0.8 copy-start.2
  368.4 3.4 copy-start.10
  375.1 104.6 %all-to-all-start.3 = ((bf16[2,32,16,1024]{3,2,0,1:T(8,128)(2,1)}), bf16[2,32,16,1024]{3,2,0,1:T(8,128)(2,1)}, u32[]{:S(2)}, u32[]{:S(2)}) async-start(bf16[2,32,16,1024]{3,2,0,1:T(8,128)(2,1)} %copy.55), calls=%async_computation.3 | async-start | bytes 4194304 | tf_op jit(solution)/shard_map/all_to_all | solution.py:71
  482.9 10.6 %copy-start.6 = (f32[2,32,8]{2,1,0:T(8,128)S(1)}, f32[2,32,8]{2,1,0:T(8,128)}, u32[]{:S(2)}) copy-start(f32[2,32,8]{2,1,0:T(8,128)} %copy.57) | copy-start | bytes 6148
  482.9 12.7 %copy-start.3 = (bf16[2,32,1024]{2,1,0:T(8,128)(2,1)S(1)}, bf16[2,32,1024]{2,1,0:T(8,128)(2,1)}, u32[]{:S(2)}) copy-start(bf16[2,32,1024]{2,1,0:T(8,128)(2,1)} %copy-done.2) | copy-start | bytes 393220
  482.9 12.7 %copy-start.5 = (bf16[1,2,32,1024]{3,2,1,0:T(8,128)(2,1)S(1)}, bf16[1,2,32,1024]{3,2,1,0:T(8,128)(2,1)}, u32[]{:S(2)}) copy-start(bf16[1,2,32,1024]{3,2,1,0:T(8,128)(2,1)} %fusion.19) | copy-start | bytes 393220
where the time goes:
time: 499 us; the launch traced here: 496 us
  blocking collectives  224 us (45%)
  waiting for transfers between devices  193 us (39%)
  local copies, waits for them, and re-layouts  36.7 us (7%)
  other arithmetic  16 us (3%)
  starting transfers between devices  13.5 us (3%)
  matrix products  12.9 us (3%)
    all_to_all x2, blocking collectives, local(): lax.all_to_all(outgoing, 'expert', split_axis=1, concat_axis=1, tiled=True)  224 us
    all_to_all x2, waiting for transfers between devices, local(): lax.all_to_all(served, 'expert', split_axis=1, concat_axis=1, tiled=True)  191 us
    gather x2, local copies, waits for them, and re-layouts, local(): jnp.take_along_axis(returned.reshape(micro_count, experts_all * capacity,...  21.1 us
    all_to_all x2, starting transfers between devices, local(): lax.all_to_all(served, 'expert', split_axis=1, concat_axis=1, tiled=True)  10.4 us
  transfers between devices with their start and end apart: 3, of which 3 were waited for; matrix products, arithmetic and copies ran while one was open for 2% of the time, Pallas kernels for 0%

commit v1 on v0

v1 whole, which is shorter than its diff:
```python
import jax
import jax.numpy as jnp
from jax import lax
from jax.sharding import PartitionSpec as P


def shifted(value, axis, by):
    size = lax.axis_size(axis)
    pairs = [(i, i + by) for i in range(size) if 0 <= i + by < size]
    return lax.ppermute(value, axis, pairs)


def normalize(inflow, gain_row):
    widened = inflow.astype(jnp.float32)
    inverse_rms = lax.rsqrt(jnp.mean(widened * widened, axis=-1, keepdims=True) + 1e-06)
    return (widened * inverse_rms * gain_row).astype(jnp.bfloat16)


def local(in_flight, arriving, norm_gain, gate_up, w_down, expert_ids, route_weights):
    experts_all = lax.axis_size("expert") * gate_up.shape[1]
    hidden_count = w_down.shape[2]
    micro_count, tokens, features = in_flight.shape[1:]
    steps = expert_ids.shape[0]
    is_first = lax.axis_index("section") == 0
    gain_row = norm_gain[0][None, None, :]
    named = expert_ids[:, 0, ..., None] == jnp.arange(experts_all, dtype=jnp.int32)
    dense = jnp.sum(jnp.where(named, route_weights[:, 0, ..., None], 0.0), axis=3)
    dense = lax.all_to_all(dense, "expert", split_axis=3, concat_axis=2, tiled=True)
    outputs = []
    inflow = in_flight[0]
    for step_number in range(steps):
        if step_number > 0:
            incoming = shifted(outputs[-1], "section", 1)
            inflow = jnp.where(is_first, arriving[step_number - 1], incoming)
        normed = normalize(inflow, gain_row)
        everyone = lax.all_gather(normed, "expert", axis=1, tiled=True)
        rows = everyone.reshape(-1, features)
        projected = jnp.dot(rows, gate_up[0, 0], preferred_element_type=jnp.float32)
        hidden = (
            jax.nn.silu(projected[:, :hidden_count]) * projected[:, hidden_count:]
        ).astype(jnp.bfloat16)
        result = jnp.dot(hidden, w_down[0, 0], preferred_element_type=jnp.float32)
        share = (result.reshape(everyone.shape) * dense[step_number]).astype(jnp.bfloat16)
        branch = lax.psum_scatter(share, "expert", scatter_dimension=1, tiled=True)
        outputs.append((inflow.astype(jnp.float32) + branch.astype(jnp.float32)).astype(jnp.bfloat16))
    return jnp.stack(outputs)[:, None]


def solution(mesh):
    return jax.shard_map(
        local,
        mesh=mesh,
        in_specs=(
            P("section", None, "expert", None),
            P(None, None, "expert", None),
            P("section", None),
            P("section", "expert", None, None),
            P("section", "expert", None, None),
            P(None, "section", None, "expert", None),
            P(None, "section", None, "expert", None),
        ),
        out_specs=P(None, "section", None, "expert", None),
        check_vma=False,
    )
```

time: 499 us -> 431 us (0.86)
  blocking collectives: 224 us -> 27.6 us
  waiting for transfers between devices: 193 us -> 341 us
  local copies, waits for them, and re-layouts: 36.7 us -> 4.02 us
  matrix products: 12.9 us -> 26.7 us
  between operations: 0.33 us -> 13.3 us
  starting transfers between devices: 13.5 us -> 2.8 us
    reduce_scatter x0 -> x2, waiting for transfers between devices: none -> 215 us  [local(): branch = lax.psum_scatter(share, 'expert', scatter_dimension=1, tiled=True)]
    all_to_all x2 -> x1, blocking collectives: 224 us -> 27.6 us  [local(): lax.all_to_all(dense, 'expert', split_axis=3, concat_axis=2, tiled=True)]
    all_to_all x2 -> x0, waiting for transfers between devices: 191 us -> none  [local(): lax.all_to_all(served, 'expert', split_axis=1, concat_axis=1, tiled=True)]
    all_gather x0 -> x2, waiting for transfers between devices: none -> 120 us  [local(): everyone = lax.all_gather(normed, 'expert', axis=1, tiled=True)]
    gather x2 -> x0, local copies, waits for them, and re-layouts: 21.1 us -> none  [local(): jnp.take_along_axis(returned.reshape(micro_count, experts_all * capacity,...]
    dot_general x6 -> x4, matrix products: 12.9 us -> 26.7 us  [the longest x2 16.8 us: local(): projected = jnp.dot(rows, gate_up[0, 0], preferred_element_type=jnp.float32)]
    all_to_all x2 -> x0, starting transfers between devices: 10.4 us -> none  [local(): lax.all_to_all(served, 'expert', split_axis=1, concat_axis=1, tiled=True)]
    all_to_all x4 -> x2, local copies, waits for them, and re-layouts: 6.99 us -> 0.51 us  [local(): lax.all_to_all(dense, 'expert', split_axis=3, concat_axis=2, tiled=True)]
  transfers between devices with their start and end apart: 3 -> 5, of which waited for: 3 -> 5; matrix products, arithmetic and copies ran while one was open for 2% -> 1% of each run, Pallas kernels for 0% -> 0%
where the time goes in v1:
time: 431 us; the launch traced here: 427 us
  waiting for transfers between devices  341 us (79%)
  blocking collectives  27.6 us (6%)
  matrix products  26.7 us (6%)
  between operations  13.3 us (3%)
  other arithmetic  12.5 us (3%)
    reduce_scatter x2, waiting for transfers between devices, local(): branch = lax.psum_scatter(share, 'expert', scatter_dimension=1, tiled=True)  215 us
    all_gather x2, waiting for transfers between devices, local(): everyone = lax.all_gather(normed, 'expert', axis=1, tiled=True)  120 us
    all_to_all x1, blocking collectives, local(): lax.all_to_all(dense, 'expert', split_axis=3, concat_axis=2, tiled=True)  27.6 us
    dot_general x2, matrix products, local(): projected = jnp.dot(rows, gate_up[0, 0], preferred_element_type=jnp.float32)  16.8 us
    dot_general x2, matrix products, local(): result = jnp.dot(hidden, w_down[0, 0], preferred_element_type=jnp.float32)  9.84 us
  transfers between devices with their start and end apart: 5, of which 5 were waited for; matrix products, arithmetic and copies ran while one was open for 1% of the time, Pallas kernels for 0%

profile of v1, /device:TPU:25, one launch (start us, length us, event | category | flops | bytes accessed | tf_op | source)
XLA Modules:
  0.0 427.4 jit_solution(6698285624427404570)
XLA Ops:
  6.5 1.2 fusion.12
  7.7 1.7 fusion.14
  9.5 0.8 copy.19
  10.2 0.8 copy.20
  11.0 0.4 select_reduce_fusion
  11.4 0.1 copy.21
  11.5 0.1 reshape.41
  11.6 27.6 %all_to_all.15 = f32[32,1,128]{2,1,0:T(1,128)S(1)} all-to-all(f32[32,1,128]{2,1,0:T(1,128)S(1)} %reshape.41), channel_id=1, replica_groups=mesh['section'=16,'expert'=32] {'expert'}, dimensions={0} | all-to-all | bytes 32768 | tf_op jit(solution)/shard_map/all_to_all | solution.py:28
  39.2 0.5 broadcast.37
  39.7 0.6 reduce
  40.3 0.1 reshape.42
  40.4 0.6 fusion.17
  41.1 0.1 mul.79
  41.2 47.1 %all-gather.3.cloned.1.call-done = bf16[2,1024,1024]{2,1,0:T(8,128)(2,1)} async-done(((bf16[2,32,1024]{2,1,0:T(8,128)(2,1)}), bf16[2,1024,1024]{2,1,0:T(8,128)(2,1)}) %all-gather.3.cloned.1.call-update) | async-done | bytes 4194320 | tf_op jit(solution)/shard_map/all_gather | solution.py:36
  88.2 8.4 %fusion.4 = f32[2048,1536]{1,0:T(8,128)S(1)} fusion(bf16[2048,1024]{1,0:T(8,128)(2,1)} %bitcast.61, bf16[1,1,1024,1536]{3,2,1,0:T(8,128)(2,1)S(1)} %copy-done), kind=kOutput, calls=%fused_computation.8 | convolution fusion | flops 6442450944 | bytes 19922944 | tf_op jit(solution)/shard_map/dot_general | solution.py:38
  96.7 2.2 fusion.1
  98.8 4.9 %multiply_convert_fusion.1 = bf16[2,1024,1024]{2,1,0:T(8,128)(2,1)} fusion(f32[2,1024]{1,0:T(2,128)S(1)} %mul.79, bf16[2,1024,768]{2,1,0:T(8,128)(2,1)S(1)} %bitcast.53, bf16[1,1,768,1024]{3,2,1,0:T(8,128)(2,1)S(1)} %copy-done.4), kind=kOutput, calls=%fused_computation.1 | convolution fusion | flops 3225419776 | bytes 8921088 | tf_op jit(solution)/shard_map/dot_general | solution.py:42
  103.8 107.3 %reduce-scatter.3.cloned.1.call-done = bf16[2,32,1024]{2,1,0:T(8,128)(2,1)} async-done(((bf16[2,1024,1024]{2,1,0:T(8,128)(2,1)}), bf16[2,32,1024]{2,1,0:T(8,128)(2,1)}) %reduce-scatter.3.cloned.1.call-update) | async-done | bytes 131088 | tf_op jit(solution)/shard_map/reduce_scatter | solution.py:44
  211.1 0.9 fusion.15
  212.0 2.7 collective-permute-start
  214.7 5.2 %collective-permute-done = bf16[2,32,1024]{2,1,0:T(8,128)(2,1)} collective-permute-done((bf16[2,32,1024]{2,1,0:T(8,128)(2,1)S(1)}, bf16[2,32,1024]{2,1,0:T(8,128)(2,1)}, u32[]{:S(2)}, u32[]{:S(2)}) %collective-permute-start) | collective-permute-done | bytes 131104 | tf_op jit(solution)/shard_map/ppermute | solution.py:10
  220.0 1.0 fusion.8
  221.0 0.8 fusion.10
  221.9 0.8 copy.23
  222.6 0.1 mul.88
  222.7 73.3 %all-gather.5.cloned.1.call-done = bf16[2,1024,1024]{2,1,0:T(8,128)(2,1)} async-done(((bf16[2,32,1024]{2,1,0:T(8,128)(2,1)}), bf16[2,1024,1024]{2,1,0:T(8,128)(2,1)}) %all-gather.5.cloned.1.call-update) | async-done | bytes 4194320 | tf_op jit(solution)/shard_map/all_gather | solution.py:36
  296.0 8.4 %fusion.2 = f32[2048,1536]{1,0:T(8,128)S(1)} fusion(bf16[2048,1024]{1,0:T(8,128)(2,1)} %bitcast.62, bf16[1,1,1024,1536]{3,2,1,0:T(8,128)(2,1)S(1)} %copy-done), kind=kOutput, calls=%fused_computation.6 | convolution fusion | flops 6442450944 | bytes 19922944 | tf_op jit(solution)/shard_map/dot_general | solution.py:38
  304.5 2.2 fusion
  306.6 4.9 %multiply_convert_fusion = bf16[2,1024,1024]{2,1,0:T(8,128)(2,1)} fusion(f32[2,1024]{1,0:T(2,128)S(1)} %mul.88, bf16[2,1024,768]{2,1,0:T(8,128)(2,1)S(1)} %bitcast.54, bf16[1,1,768,1024]{3,2,1,0:T(8,128)(2,1)S(1)} %copy-done.5), kind=kOutput, calls=%fused_computation | convolution fusion | flops 3225419776 | bytes 8921088 | tf_op jit(solution)/shard_map/dot_general | solution.py:42
  311.6 107.6 %reduce-scatter.5.cloned.1.call-done = bf16[2,32,1024]{2,1,0:T(8,128)(2,1)} async-done(((bf16[2,1024,1024]{2,1,0:T(8,128)(2,1)}), bf16[2,32,1024]{2,1,0:T(8,128)(2,1)}) %reduce-scatter.5.cloned.1.call-update) | async-done | bytes 131088 | tf_op jit(solution)/shard_map/reduce_scatter | solution.py:44
  419.2 0.9 fusion.16
  420.1 0.7 maximum_bitcast_fusion
  (24 shorter events, 0.2 us)
Async XLA Ops:
  6.5 81.7 %copy-start = (bf16[1,1,1024,1536]{3,2,1,0:T(8,128)(2,1)S(1)}, bf16[1,1,1024,1536]{3,2,1,0:T(8,128)(2,1)}, u32[]{:S(2)}) copy-start(bf16[1,1,1024,1536]{3,2,1,0:T(8,128)(2,1)} %param.10) | copy-start | bytes 9437188
  6.5 81.7 %all-gather.3.cloned.1.call-start = ((), (), s32[]{:S(2)}) async-start(), calls=%async_computation.3 | async-start | bytes 4325376 | tf_op jit(solution)/shard_map/all_gather | solution.py:36
  9.4 201.7 %reduce-scatter.3.cloned.1.call-start = ((), (), s32[]{:S(2)}) async-start(), calls=%async_computation.4 | async-start | bytes 4325376 | tf_op jit(solution)/shard_map/reduce_scatter | solution.py:44
  96.6 2.2 copy-start.4
  103.8 107.3 %copy-start.1 = (bf16[1,2,32,1024]{3,2,1,0:T(8,128)(2,1)S(1)}, bf16[1,2,32,1024]{3,2,1,0:T(8,128)(2,1)}, u32[]{:S(2)}) copy-start(bf16[1,2,32,1024]{3,2,1,0:T(8,128)(2,1)} %param.7) | copy-start | bytes 393220
  103.8 116.2 %copy-start.2 = (bf16[1,2,32,1024]{3,2,1,0:T(8,128)(2,1)S(1)}, bf16[1,2,32,1024]{3,2,1,0:T(8,128)(2,1)}, u32[]{:S(2)}) copy-start(bf16[1,2,32,1024]{3,2,1,0:T(8,128)(2,1)} %param.8) | copy-start | bytes 393220
  103.8 117.3 %copy-start.3 = (f32[1,1024]{1,0:T(1,128)S(1)}, f32[1,1024]{1,0:T(1,128)}, u32[]{:S(2)}) copy-start(f32[1,1024]{1,0:T(1,128)} %param.9) | copy-start | bytes 12292
  103.8 192.2 %all-gather.5.cloned.1.call-start = ((), (), s32[]{:S(2)}) async-start(), calls=%async_computation.5 | async-start | bytes 4325376 | tf_op jit(solution)/shard_map/all_gather | solution.py:36
  212.0 7.9 %collective-permute-start = (bf16[2,32,1024]{2,1,0:T(8,128)(2,1)S(1)}, bf16[2,32,1024]{2,1,0:T(8,128)(2,1)}, u32[]{:S(2)}, u32[]{:S(2)}) collective-permute-start(bf16[2,32,1024]{2,1,0:T(8,128)(2,1)S(1)} %fusion.15), channel_id=1, source_target_pairs={{0,32},{32,64},{64,96},{96,128},{128,160},{160,192},{192,224},{224... | collective-permute-start | bytes 393224 | tf_op jit(solution)/shard_map/ppermute | solution.py:10
  221.8 197.4 %reduce-scatter.5.cloned.1.call-start = ((), (), s32[]{:S(2)}) async-start(), calls=%async_computation.6 | async-start | bytes 4325376 | tf_op jit(solution)/shard_map/reduce_scatter | solution.py:44
  304.5 2.2 copy-start.5
Sparse Core Ops, SparseCore 0:
  9.5 78.6 all-gather.2
  103.9 107.1 reduce-scatter.2
  221.9 74.0 all-gather.4
  311.7 107.4 reduce-scatter.4

commit v2 on v1

v2 whole, which is shorter than its diff:
```python
import functools

import jax
import jax.numpy as jnp
from jax import lax
from jax.experimental import pallas as pl
from jax.experimental.pallas import tpu as pltpu
from jax.sharding import PartitionSpec as P

MESH = pl.DeviceIdType.MESH
LANES = 128


def relay_kernel(
    chips,
    sections,
    in_flight,
    arriving,
    norm_gain,
    gate_up,
    w_down,
    expert_ids,
    route_weights,
    out,
    rows0,
    rows1,
    sum_in,
    sum_out,
    part_out,
    part_in,
    own,
    home,
    inflow,
    entering,
    shifted,
    results,
    hidden,
    shares,
    gain,
    up_weights,
    down_weights,
    ids,
    weights,
    load_sems,
    swap_send,
    swap_recv,
    row_send,
    row_recv,
    mate_send,
    mate_recv,
    sum_send,
    sum_recv,
    part_send,
    part_recv,
    shift_send,
    shift_recv,
    out_send,
    out_recv,
    out_sems,
):
    steps, micros, tokens, top_count = expert_ids.shape[0], *expert_ids.shape[2:]
    features = in_flight.shape[-1]
    ff = w_down.shape[2]
    group = 2 * tokens
    tile = min(256, ff)
    experts = 2 * chips

    me = lax.axis_index("expert")
    section = lax.axis_index("section")
    core = lax.rem(me, 2)
    mate = me + 1 - 2 * core
    ahead = lax.rem(me + 2 - 4 * core + experts, experts)
    behind = lax.rem(me - 2 + 4 * core + experts, experts)
    section_after = lax.rem(section + 1, sections)
    section_before = lax.rem(section + sections - 1, sections)
    mine = pl.ds(pl.multiple_of(core * tokens, tokens), tokens)
    other = pl.ds(pl.multiple_of((1 - core) * tokens, tokens), tokens)

    loads = [
        pltpu.make_async_copy(source, target, load_sems.at[i])
        for i, (source, target) in enumerate(
            (
                (expert_ids, ids),
                (route_weights, weights),
                (norm_gain, gain),
                (in_flight.at[0, core], inflow.at[0, mine]),
                (arriving.at[0, core], entering.at[mine]),
                (gate_up.at[0, 0], up_weights),
                (w_down.at[0, 0], down_weights),
            )
        )
    ]
    for load in loads:
        load.start()

    barrier = pltpu.get_barrier_semaphore()
    for neighbour in (ahead, behind, mate):
        pl.semaphore_signal(barrier, inc=1, device_id={"expert": neighbour}, device_id_type=MESH)
    for neighbour in (section_after, section_before):
        pl.semaphore_signal(barrier, inc=1, device_id={"section": neighbour}, device_id_type=MESH)

    loads[0].wait()
    loads[1].wait()
    lane = lax.broadcasted_iota(jnp.int32, (tokens, LANES), 1)
    for micro in range(micros):
        dense = []
        for step in range(steps):
            step_ids, step_weights = ids[step, 0, micro], weights[step, 0, micro]
            total = jnp.zeros((tokens, LANES), jnp.float32)
            for k in range(top_count):
                named = step_ids[:, k : k + 1] == lax.rem(lane, experts)
                total = total + jnp.where(named, step_weights[:, k : k + 1], 0.0)
            dense.append(total)
        both = jnp.where(lane < 2 * experts, dense[0], dense[1])
        high = both.astype(jnp.bfloat16).astype(jnp.float32)
        is_high = lax.rem(lane, 2 * experts) < experts
        shares[micro] = jnp.where(is_high, high, both - high).astype(jnp.bfloat16)

    pl.semaphore_wait(barrier, 5)

    def swap(index, source, target):
        return pltpu.make_async_remote_copy(
            source, target, swap_send.at[index], swap_recv.at[index], {"expert": mate}, MESH
        )

    swaps = (
        swap(0, in_flight.at[0, 1 - core], inflow.at[0, mine]),
        swap(1, shares.at[1 - core], rows0.at[0, mine, pl.ds(features, LANES)]),
        swap(2, arriving.at[0, 1 - core], entering.at[mine]),
    )
    for copy in swaps:
        copy.start()
    rows0[0, mine, pl.ds(features, LANES)] = shares[core]
    sum_in[:, 1] = jnp.zeros((steps,) + sum_in.shape[2:], sum_in.dtype)

    mate_lane = lax.broadcasted_iota(jnp.int32, (2 * group, LANES), 1)

    def relay_step(step, rows):
        width = rows.shape[-1]

        def pass_on(k):
            return pltpu.make_async_remote_copy(
                rows.at[k, pl.ds(0, group)],
                rows.at[k + 1, pl.ds(0, group)],
                row_send.at[step],
                row_recv.at[step, k + 1],
                {"expert": ahead},
                MESH,
            )

        def to_mate(k):
            return pltpu.make_async_remote_copy(
                rows.at[k, pl.ds(0, group)],
                rows.at[k, pl.ds(group, group)],
                mate_send.at[step],
                mate_recv.at[step, k],
                {"expert": mate},
                MESH,
            )

        def part_to_mate(k):
            return pltpu.make_async_remote_copy(
                part_out.at[step, k],
                part_in.at[step, k],
                part_send.at[step],
                part_recv.at[step, k],
                {"expert": mate},
                MESH,
            )

        def sum_on(k):
            return pltpu.make_async_remote_copy(
                sum_out.at[step, k],
                sum_in.at[step, k + 1],
                sum_send.at[step],
                sum_recv.at[step, k + 1],
                {"expert": ahead},
                MESH,
            )

        def forward(k):
            @pl.when(k < chips - 1)
            def _():
                pass_on(k).start()

            to_mate(k).start()

        def multiply(k):
            to_mate(k).wait_recv()
            slot = lax.rem(k, 2)
            at = step * 2 * experts + me
            picked = (mate_lane == at) | (mate_lane == at + experts)
            share = rows0[k, :, pl.ds(features, LANES)].astype(jnp.float32)
            share = jnp.sum(jnp.where(picked, share, 0.0), axis=1, keepdims=True)
            block = rows[k, :, pl.ds(0, features)]
            for start in range(0, ff, tile):
                gate = jnp.dot(
                    block, up_weights[:, start : start + tile], preferred_element_type=jnp.float32
                )
                lift = jnp.dot(
                    block,
                    up_weights[:, ff + start : ff + start + tile],
                    preferred_element_type=jnp.float32,
                )
                hidden[:, start : start + tile] = (gate / (1.0 + jnp.exp(-gate)) * lift).astype(
                    jnp.bfloat16
                )
            for start in range(0, features, tile):
                result = jnp.dot(
                    hidden[...],
                    down_weights[:, start : start + tile],
                    preferred_element_type=jnp.float32,
                )
                result = result.astype(jnp.bfloat16).astype(jnp.float32) * share
                own[slot, :, start : start + tile] = result[:group]
                part_out[step, k, :, start : start + tile] = result[group:].astype(jnp.bfloat16)
            part_to_mate(k).start()

        def add(k):
            part_to_mate(k).wait_recv()
            slot = lax.rem(k, 2)
            both = own[slot] + part_in[step, k].astype(jnp.float32)

            @pl.when(k == 0)
            def _():
                home[...] = both + inflow[step].astype(jnp.float32)

            @pl.when(k > 0)
            def _():
                @pl.when(k > 1)
                def _():
                    sum_on(k - 1).wait_recv()

                sum_out[step, k] = (both + sum_in[step, k].astype(jnp.float32)).astype(jnp.bfloat16)
                sum_on(k).start()

        forward(0)

        def turn(k, carry):
            @pl.when(k < chips)
            def _():
                pass_on(k - 1).wait_recv()
                forward(k)

            multiply(k - 1)

            @pl.when(k > 1)
            def _():
                add(k - 2)

            return carry

        lax.fori_loop(1, chips + 1, turn, 0)
        add(chips - 1)
        sum_on(chips - 1).wait_recv()
        results[step] = (home[...] + sum_in[step, chips].astype(jnp.float32)).astype(jnp.bfloat16)

    def normalize(step, rows):
        wide = inflow[step].astype(jnp.float32)
        inverse = lax.rsqrt(jnp.mean(wide * wide, axis=-1, keepdims=True) + 1e-06)
        rows[0, pl.ds(0, group), pl.ds(0, features)] = (wide * inverse * gain[...]).astype(
            jnp.bfloat16
        )

    def hand_out(step):
        local = pltpu.make_async_copy(
            results.at[step, mine], out.at[step, 0, core], out_sems.at[step]
        )
        remote = pltpu.make_async_remote_copy(
            results.at[step, other],
            out.at[step, 0, core],
            out_send.at[step],
            out_recv.at[step],
            {"expert": mate},
            MESH,
        )
        return local, remote

    loads[2].wait()
    loads[3].wait()
    swaps[0].wait_recv()
    swaps[1].wait_recv()
    normalize(0, rows0)
    for load in loads[4:]:
        load.wait()
    relay_step(0, rows0)
    relay = pltpu.make_async_remote_copy(
        results.at[0], shifted, shift_send, shift_recv, {"section": section_after}, MESH
    )
    relay.start()
    for copy in hand_out(0):
        copy.start()
    swaps[2].wait_recv()
    relay.wait_recv()
    inflow[1] = jnp.where(section == 0, entering[...], shifted[...])
    normalize(1, rows1)
    relay_step(1, rows1)
    for copy in hand_out(1):
        copy.start()

    for copy in swaps:
        copy.wait_send()
    relay.wait_send()
    for step, rows in enumerate((rows0, rows1)):

        def drain(source, sem):
            pltpu.make_async_copy(source, source, sem).wait()

        drain(rows.at[pl.ds(0, chips - 1), pl.ds(0, group)], row_send.at[step])
        drain(rows.at[pl.ds(0, chips), pl.ds(0, group)], mate_send.at[step])
        drain(part_out.at[step], part_send.at[step])
        drain(sum_out.at[step, pl.ds(1, chips - 1)], sum_send.at[step])
        local, remote = hand_out(step)
        local.wait()
        remote.wait()


def local(in_flight, arriving, norm_gain, gate_up, w_down, expert_ids, route_weights):
    sections, chips = lax.axis_size("section"), lax.axis_size("expert") // 2
    _, micros, tokens, features = in_flight.shape
    steps = expert_ids.shape[0]
    ff = w_down.shape[2]
    group = 2 * tokens
    half, full = jnp.bfloat16, jnp.float32
    dma = pltpu.SemaphoreType.DMA
    block = (group, features)
    anywhere = pl.BlockSpec(memory_space=pl.ANY)
    return pl.pallas_call(
        functools.partial(relay_kernel, chips, sections),
        out_shape=jax.ShapeDtypeStruct((steps, 1, micros, tokens, features), half),
        in_specs=[anywhere] * 7,
        out_specs=anywhere,
        scratch_shapes=[
            pltpu.VMEM((chips, 2 * group, features + LANES), half),
            pltpu.VMEM((chips, 2 * group, features), half),
            pltpu.VMEM((steps, chips + 1) + block, half),
            pltpu.VMEM((steps, chips) + block, half),
            pltpu.VMEM((steps, chips) + block, half),
            pltpu.VMEM((steps, chips) + block, half),
            pltpu.VMEM((2,) + block, full),
            pltpu.VMEM(block, full),
            pltpu.VMEM((steps,) + block, half),
            pltpu.VMEM(block, half),
            pltpu.VMEM(block, half),
            pltpu.VMEM((steps,) + block, half),
            pltpu.VMEM((2 * group, ff), half),
            pltpu.VMEM((micros, tokens, LANES), half),
            pltpu.VMEM((1, features), full),
            pltpu.VMEM(gate_up.shape[2:], half),
            pltpu.VMEM(w_down.shape[2:], half),
            pltpu.VMEM(expert_ids.shape, jnp.int32),
            pltpu.VMEM(route_weights.shape, full),
            dma((7,)),
            dma((3,)),
            dma((3,)),
            dma((steps,)),
            dma((steps, chips)),
            dma((steps,)),
            dma((steps, chips)),
            dma((steps,)),
            dma((steps, chips + 1)),
            dma((steps,)),
            dma((steps, chips)),
            dma,
            dma,
            dma((steps,)),
            dma((steps,)),
            dma((steps,)),
        ],
        compiler_params=pltpu.CompilerParams(
            collective_id=0, has_side_effects=True, vmem_limit_bytes=56 * 2**20
        ),
        name="relay",
    )(in_flight, arriving, norm_gain, gate_up, w_down, expert_ids, route_weights)


def solution(mesh):
    return jax.shard_map(
        local,
        mesh=mesh,
        in_specs=(
            P("section", None, "expert", None),
            P(None, None, "expert", None),
            P("section", None),
            P("section", "expert", None, None),
            P("section", "expert", None, None),
            P(None, "section", None, "expert", None),
            P(None, "section", None, "expert", None),
        ),
        out_specs=P(None, "section", None, "expert", None),
        check_vma=False,
    )
```

time: 431 us -> 182 us (0.42)
  waiting for transfers between devices: 341 us -> 0 us
  Pallas kernels: 0 us -> 174 us
  blocking collectives: 27.6 us -> 0 us
  matrix products: 26.7 us -> 0 us
  between operations: 13.3 us -> 0.01 us
  other arithmetic: 12.5 us -> 0 us
    reduce_scatter x2 -> x0, waiting for transfers between devices: 215 us -> none  [local(): branch = lax.psum_scatter(share, 'expert', scatter_dimension=1, tiled=True)]
    pallas_call x0 -> x1, Pallas kernels: none -> 174 us  [local(): pl.pallas_call(functools.partial(relay_kernel, chips, sections), out_shap...]
    all_gather x2 -> x0, waiting for transfers between devices: 120 us -> none  [local(): everyone = lax.all_gather(normed, 'expert', axis=1, tiled=True)]
    all_to_all x1 -> x0, blocking collectives: 27.6 us -> none  [local(): lax.all_to_all(dense, 'expert', split_axis=3, concat_axis=2, tiled=True)]
    dot_general x4 -> x0, matrix products: 26.7 us -> none  [the longest x2 16.8 us: local(): projected = jnp.dot(rows, gate_up[0, 0], preferred_element_type=jnp.float32)]
    convert_element_type x5 -> x0, other arithmetic: 7.68 us -> none  [the longest x2 4.32 us: local(): hidden = (jax.nn.silu(projected[:, :hidden_count]) * projected[:, hidden_...]
    ppermute x1 -> x0, waiting for transfers between devices: 5.25 us -> none  [shifted(): return lax.ppermute(value, axis, pairs)]
  transfers between devices with their start and end apart: 5 -> 0, of which waited for: 5 -> 0; matrix products, arithmetic and copies ran while one was open for 1% -> 0% of each run, Pallas kernels for 0% -> 0%
where the time goes in v2:
time: 182 us; the launch traced here: 179 us
  Pallas kernels  174 us (96%)
  local copies, waits for them, and re-layouts  4.51 us (2%)
    pallas_call x1, Pallas kernels, local(): pl.pallas_call(functools.partial(relay_kernel, chips, sections), out_shap...  174 us
    unnamed x3, local copies, waits for them, and re-layouts  4.51 us

profile of v2, /device:TPU:25, one launch (start us, length us, event | category | flops | bytes accessed | tf_op | source)
XLA Modules:
  0.0 178.6 jit_solution(743171058701866033)
XLA Ops:
  0.0 1.4 copy.8.expert_ids
  1.4 1.4 copy.9.route_weights
  2.8 174.1 %relay.1 = bf16[2,1,2,32,1024]{4,3,2,1,0:T(8,128)(2,1)} custom-call(bf16[1,2,32,1024]{3,2,1,0:T(8,128)(2,1)} %in_flight.1, bf16[1,2,32,1024]{3,2,1,0:T(8,128)(2,1)} %arriving.1, f32[1,1024]{1,0:T(1,128)} %norm_gain.1, bf16[1,1,1024,1536]{3,2,1,0:T(8,128)(2,1)} %gate_up.1, bf16[1,1,768,1024]{3,2,1,0:T(8,128)(2,1)} %w_down.1, ...), custom_call_target="tpu_custom_call" | custom-call | tf_op jit(solution)/shard_map/relay/pallas_call | solution.py:328
  177.0 1.7 copy.11

commit v3 on v2

--- a/solution.py
+++ b/solution.py
@@ -9,6 +9,7 @@
 
 MESH = pl.DeviceIdType.MESH
 LANES = 128
+CHUNK = 16
 
 
 def relay_kernel(
@@ -58,19 +59,25 @@
     out_recv,
     out_sems,
 ):
-    steps, micros, tokens, top_count = expert_ids.shape[0], *expert_ids.shape[2:]
+    steps, micros, top_count, tokens = expert_ids.shape[0], *expert_ids.shape[2:]
     features = in_flight.shape[-1]
     ff = w_down.shape[2]
     group = 2 * tokens
     tile = min(256, ff)
     experts = 2 * chips
+    chunks = [pl.ds(start, CHUNK) for start in range(0, group, CHUNK)]
 
     me = lax.axis_index("expert")
     section = lax.axis_index("section")
-    core = lax.rem(me, 2)
+    chip, core = me // 2, lax.rem(me, 2)
     mate = me + 1 - 2 * core
-    ahead = lax.rem(me + 2 - 4 * core + experts, experts)
-    behind = lax.rem(me - 2 + 4 * core + experts, experts)
+    role = lax.rem(core + chip, 2)
+
+    def on_ring(distance):
+        there = lax.rem(chip + distance * (1 - 2 * role) + chips, chips)
+        return 2 * there + lax.rem(role + there, 2)
+
+    ahead, behind = on_ring(1), on_ring(-1)
     section_after = lax.rem(section + 1, sections)
     section_before = lax.rem(section + sections - 1, sections)
     mine = pl.ds(pl.multiple_of(core * tokens, tokens), tokens)
@@ -83,8 +90,8 @@
                 (expert_ids, ids),
                 (route_weights, weights),
                 (norm_gain, gain),
-                (in_flight.at[0, core], inflow.at[0, mine]),
-                (arriving.at[0, core], entering.at[mine]),
+                (in_flight.at[0, role], inflow.at[0, mine]),
+                (arriving.at[0, role], entering.at[mine]),
                 (gate_up.at[0, 0], up_weights),
                 (w_down.at[0, 0], down_weights),
             )
@@ -101,20 +108,20 @@
 
     loads[0].wait()
     loads[1].wait()
-    lane = lax.broadcasted_iota(jnp.int32, (tokens, LANES), 1)
+    line = lax.broadcasted_iota(jnp.int32, (LANES, tokens), 0)
+    is_high = lax.rem(line, 2 * experts) < experts
     for micro in range(micros):
         dense = []
         for step in range(steps):
             step_ids, step_weights = ids[step, 0, micro], weights[step, 0, micro]
-            total = jnp.zeros((tokens, LANES), jnp.float32)
+            total = jnp.zeros((LANES, tokens), jnp.float32)
             for k in range(top_count):
-                named = step_ids[:, k : k + 1] == lax.rem(lane, experts)
-                total = total + jnp.where(named, step_weights[:, k : k + 1], 0.0)
+                named = step_ids[k : k + 1] == lax.rem(line, experts)
+                total = total + jnp.where(named, step_weights[k : k + 1], 0.0)
             dense.append(total)
-        both = jnp.where(lane < 2 * experts, dense[0], dense[1])
+        both = jnp.where(line < 2 * experts, dense[0], dense[1])
         high = both.astype(jnp.bfloat16).astype(jnp.float32)
-        is_high = lax.rem(lane, 2 * experts) < experts
-        shares[micro] = jnp.where(is_high, high, both - high).astype(jnp.bfloat16)
+        shares[micro] = jnp.where(is_high, high, both - high).T.astype(jnp.bfloat16)
 
     pl.semaphore_wait(barrier, 5)
 
@@ -124,13 +131,13 @@
         )
 
     swaps = (
-        swap(0, in_flight.at[0, 1 - core], inflow.at[0, mine]),
-        swap(1, shares.at[1 - core], rows0.at[0, mine, pl.ds(features, LANES)]),
-        swap(2, arriving.at[0, 1 - core], entering.at[mine]),
+        swap(0, in_flight.at[0, 1 - role], inflow.at[0, mine]),
+        swap(1, shares.at[1 - role], rows0.at[0, mine, pl.ds(features, LANES)]),
+        swap(2, arriving.at[0, 1 - role], entering.at[mine]),
     )
     for copy in swaps:
         copy.start()
-    rows0[0, mine, pl.ds(features, LANES)] = shares[core]
+    rows0[0, mine, pl.ds(features, LANES)] = shares[role]
     sum_in[:, 1] = jnp.zeros((steps,) + sum_in.shape[2:], sum_in.dtype)
 
     mate_lane = lax.broadcasted_iota(jnp.int32, (2 * group, LANES), 1)
@@ -138,12 +145,12 @@
     def relay_step(step, rows):
         width = rows.shape[-1]
 
-        def pass_on(k):
+        def pass_on(k, i):
             return pltpu.make_async_remote_copy(
-                rows.at[k, pl.ds(0, group)],
-                rows.at[k + 1, pl.ds(0, group)],
+                rows.at[k, chunks[i]],
+                rows.at[k + 1, chunks[i]],
                 row_send.at[step],
-                row_recv.at[step, k + 1],
+                row_recv.at[step, k + 1, i],
                 {"expert": ahead},
                 MESH,
             )
@@ -168,30 +175,25 @@
                 MESH,
             )
 
-        def sum_on(k):
+        def sum_on(k, i):
             return pltpu.make_async_remote_copy(
-                sum_out.at[step, k],
-                sum_in.at[step, k + 1],
+                sum_out.at[step, k, chunks[i]],
+                sum_in.at[step, k + 1, chunks[i]],
                 sum_send.at[step],
-                sum_recv.at[step, k + 1],
+                sum_recv.at[step, k + 1, i],
                 {"expert": ahead},
                 MESH,
             )
 
-        def forward(k):
+        def forward(k, i):
+            pass_on(k - 1, i).wait_recv()
+
             @pl.when(k < chips - 1)
             def _():
-                pass_on(k).start()
-
-            to_mate(k).start()
-
-        def multiply(k):
+                pass_on(k, i).start()
+
+        def multiply_up(k):
             to_mate(k).wait_recv()
-            slot = lax.rem(k, 2)
-            at = step * 2 * experts + me
-            picked = (mate_lane == at) | (mate_lane == at + experts)
-            share = rows0[k, :, pl.ds(features, LANES)].astype(jnp.float32)
-            share = jnp.sum(jnp.where(picked, share, 0.0), axis=1, keepdims=True)
             block = rows[k, :, pl.ds(0, features)]
             for start in range(0, ff, tile):
                 gate = jnp.dot(
@@ -205,6 +207,13 @@
                 hidden[:, start : start + tile] = (gate / (1.0 + jnp.exp(-gate)) * lift).astype(
                     jnp.bfloat16
                 )
+
+        def multiply_down(k):
+            slot = lax.rem(k, 2)
+            at = step * 2 * experts + me
+            picked = (mate_lane == at) | (mate_lane == at + experts)
+            share = rows0[k, :, pl.ds(features, LANES)].astype(jnp.float32)
+            share = jnp.sum(jnp.where(picked, share, 0.0), axis=1, keepdims=True)
             for start in range(0, features, tile):
                 result = jnp.dot(
                     hidden[...],
@@ -216,59 +225,98 @@
                 part_out[step, k, :, start : start + tile] = result[group:].astype(jnp.bfloat16)
             part_to_mate(k).start()
 
-        def add(k):
-            part_to_mate(k).wait_recv()
-            slot = lax.rem(k, 2)
-            both = own[slot] + part_in[step, k].astype(jnp.float32)
-
-            @pl.when(k == 0)
-            def _():
-                home[...] = both + inflow[step].astype(jnp.float32)
-
-            @pl.when(k > 0)
-            def _():
-                @pl.when(k > 1)
-                def _():
-                    sum_on(k - 1).wait_recv()
-
-                sum_out[step, k] = (both + sum_in[step, k].astype(jnp.float32)).astype(jnp.bfloat16)
-                sum_on(k).start()
-
-        forward(0)
-
-        def turn(k, carry):
-            @pl.when(k < chips)
-            def _():
-                pass_on(k - 1).wait_recv()
-                forward(k)
-
-            multiply(k - 1)
-
+        def add(k, i):
             @pl.when(k > 1)
             def _():
-                add(k - 2)
+                sum_on(k - 1, i).wait_recv()
+
+            rows_now = chunks[i]
+            total = own[lax.rem(k, 2), rows_now] + part_in[step, k, rows_now].astype(jnp.float32)
+            total = total + sum_in[step, k, rows_now].astype(jnp.float32)
+            sum_out[step, k, rows_now] = total.astype(jnp.bfloat16)
+            sum_on(k, i).start()
+
+        def turn(k, carry):
+            for i in range(len(chunks)):
+
+                @pl.when(k < chips)
+                def _():
+                    forward(k, i)
+
+                if i < len(chunks) - 1:
+
+                    @pl.when(k > 2)
+                    def _():
+                        add(k - 2, i + 1)
+
+                    if i == 0:
+                        multiply_up(k - 1)
+                    elif i == 1:
+                        multiply_down(k - 1)
+                else:
+
+                    @pl.when(k < chips)
+                    def _():
+                        to_mate(k).start()
+
+                    part_to_mate(k - 1).wait_recv()
+
+                    @pl.when(k > 1)
+                    def _():
+                        add(k - 1, 0)
+
+                    @pl.when(k == 1)
+                    def _():
+                        home[...] = (
+                            own[0]
+                            + part_in[step, 0].astype(jnp.float32)
+                            + inflow[step].astype(jnp.float32)
+                        )
 
             return carry
 
+        for i, rows_now in enumerate(chunks):
+            prepare(step, rows, rows_now, i)
+            pass_on(0, i).start()
+        to_mate(0).start()
+        if step == 0:
+            loads[5].wait()
+            loads[6].wait()
         lax.fori_loop(1, chips + 1, turn, 0)
-        add(chips - 1)
-        sum_on(chips - 1).wait_recv()
-        results[step] = (home[...] + sum_in[step, chips].astype(jnp.float32)).astype(jnp.bfloat16)
-
-    def normalize(step, rows):
-        wide = inflow[step].astype(jnp.float32)
+        for i in range(1, len(chunks)):
+            add(chips - 1, i)
+        for i, rows_now in enumerate(chunks):
+            sum_on(chips - 1, i).wait_recv()
+            last = sum_in[step, chips, rows_now].astype(jnp.float32)
+            results[step, rows_now] = (home[rows_now] + last).astype(jnp.bfloat16)
+            if step + 1 < steps:
+                relay(i).start()
+
+    def relay(i):
+        return pltpu.make_async_remote_copy(
+            results.at[0, chunks[i]],
+            shifted.at[chunks[i]],
+            shift_send,
+            shift_recv.at[i],
+            {"section": section_after},
+            MESH,
+        )
+
+    def prepare(step, rows, rows_now, i):
+        if step > 0:
+            relay(i).wait_recv()
+            inflow[step, rows_now] = jnp.where(section == 0, entering[rows_now], shifted[rows_now])
+        wide = inflow[step, rows_now].astype(jnp.float32)
         inverse = lax.rsqrt(jnp.mean(wide * wide, axis=-1, keepdims=True) + 1e-06)
-        rows[0, pl.ds(0, group), pl.ds(0, features)] = (wide * inverse * gain[...]).astype(
-            jnp.bfloat16
-        )
+        rows[0, rows_now, pl.ds(0, features)] = (wide * inverse * gain[...]).astype(jnp.bfloat16)
 
     def hand_out(step):
         local = pltpu.make_async_copy(
-            results.at[step, mine], out.at[step, 0, core], out_sems.at[step]
+            results.at[step, mine], out.at[step, 0, role], out_sems.at[step]
         )
         remote = pltpu.make_async_remote_copy(
             results.at[step, other],
-            out.at[step, 0, core],
+            out.at[step, 0, role],
             out_send.at[step],
             out_recv.at[step],
             {"expert": mate},
@@ -280,32 +328,23 @@
     loads[3].wait()
     swaps[0].wait_recv()
     swaps[1].wait_recv()
-    normalize(0, rows0)
-    for load in loads[4:]:
-        load.wait()
     relay_step(0, rows0)
-    relay = pltpu.make_async_remote_copy(
-        results.at[0], shifted, shift_send, shift_recv, {"section": section_after}, MESH
-    )
-    relay.start()
     for copy in hand_out(0):
         copy.start()
+    loads[4].wait()
     swaps[2].wait_recv()
-    relay.wait_recv()
-    inflow[1] = jnp.where(section == 0, entering[...], shifted[...])
-    normalize(1, rows1)
     relay_step(1, rows1)
     for copy in hand_out(1):
         copy.start()
 
     for copy in swaps:
         copy.wait_send()
-    relay.wait_send()
+
+    def drain(source, sem):
+        pltpu.make_async_copy(source, source, sem).wait()
+
+    drain(results.at[0], shift_send)
     for step, rows in enumerate((rows0, rows1)):
-
-        def drain(source, sem):
-            pltpu.make_async_copy(source, source, sem).wait()
-
         drain(rows.at[pl.ds(0, chips - 1), pl.ds(0, group)], row_send.at[step])
         drain(rows.at[pl.ds(0, chips), pl.ds(0, group)], mate_send.at[step])
         drain(part_out.at[step], part_send.at[step])
@@ -321,6 +360,7 @@
     steps = expert_ids.shape[0]
     ff = w_down.shape[2]
     group = 2 * tokens
+    expert_ids, route_weights = expert_ids.swapaxes(3, 4), route_weights.swapaxes(3, 4)
     half, full = jnp.bfloat16, jnp.float32
     dma = pltpu.SemaphoreType.DMA
     block = (group, features)
@@ -354,15 +394,15 @@
             dma((3,)),
             dma((3,)),
             dma((steps,)),
+            dma((steps, chips, group // CHUNK)),
+            dma((steps,)),
             dma((steps, chips)),
             dma((steps,)),
-            dma((steps, chips)),
-            dma((steps,)),
-            dma((steps, chips + 1)),
+            dma((steps, chips + 1, group // CHUNK)),
             dma((steps,)),
             dma((steps, chips)),
             dma,
-            dma,
+            dma((group // CHUNK,)),
             dma((steps,)),
             dma((steps,)),
             dma((steps,)),

time: 182 us -> 136 us (0.75)
  the two profiles are of different devices: /device:TPU:25 before, /device:TPU:1 now
where the time goes in v3:
time: 136 us
  Pallas kernels  134 us (99%)
  local copies, waits for them, and re-layouts  1.67 us (1%)
    pallas_call x1, Pallas kernels, local(): pl.pallas_call(functools.partial(relay_kernel, chips, sections), out_shap...  134 us

profile of v3, /device:TPU:1, one launch (start us, length us, event | category | flops | bytes accessed | tf_op | source)
XLA Modules:
  0.0 136.0 jit_solution(9696684694826524476)
XLA Ops:
  0.0 134.3 %relay.1 = bf16[2,1,2,32,1024]{4,3,2,1,0:T(8,128)(2,1)} custom-call(bf16[1,2,32,1024]{3,2,1,0:T(8,128)(2,1)} %in_flight.1, bf16[1,2,32,1024]{3,2,1,0:T(8,128)(2,1)} %arriving.1, f32[1,1024]{1,0:T(1,128)} %norm_gain.1, bf16[1,1,1024,1536]{3,2,1,0:T(8,128)(2,1)} %gate_up.1, bf16[1,1,768,1024]{3,2,1,0:T(8,128)(2,1)} %w_down.1, s32[2,1,2,8,32]{4,3,2,1,0:T(8,128)} %bitcast.2, ...), custom_call_target="tpu_custom_call" | custom-call | tf_op jit(solution)/shard_map/relay/pallas_call | solution.py:368
  134.3 1.7 %copy.9 = bf16[2,1,2,32,1024]{4,3,2,1,0:T(8,128)(2,1)} copy(bf16[2,1,2,32,1024]{4,3,2,1,0:T(8,128)(2,1)} %relay.1) | data formatting | bytes 524288

commit v4 on v3

--- a/solution.py
+++ b/solution.py
@@ -31,10 +31,14 @@
     part_in,
     own,
     home,
+    home_before,
+    home_mate,
     inflow,
     entering,
-    shifted,
-    results,
+    sum_before,
+    sum_last,
+    first,
+    last,
     hidden,
     shares,
     gain,
@@ -53,8 +57,12 @@
     sum_recv,
     part_send,
     part_recv,
-    shift_send,
-    shift_recv,
+    home_send,
+    home_recv,
+    before_send,
+    before_recv,
+    last_send,
+    last_recv,
     out_send,
     out_recv,
     out_sems,
@@ -65,7 +73,9 @@
     group = 2 * tokens
     tile = min(256, ff)
     experts = 2 * chips
+    mine, other, block = pl.ds(0, tokens), pl.ds(tokens, tokens), pl.ds(0, group)
     chunks = [pl.ds(start, CHUNK) for start in range(0, group, CHUNK)]
+    half = len(chunks) // 2
 
     me = lax.axis_index("expert")
     section = lax.axis_index("section")
@@ -78,19 +88,31 @@
         return 2 * there + lax.rem(role + there, 2)
 
     ahead, behind = on_ring(1), on_ring(-1)
-    section_after = lax.rem(section + 1, sections)
-    section_before = lax.rem(section + sections - 1, sections)
-    mine = pl.ds(pl.multiple_of(core * tokens, tokens), tokens)
-    other = pl.ds(pl.multiple_of((1 - core) * tokens, tokens), tokens)
+    ahead_mate = ahead + 1 - 2 * lax.rem(ahead, 2)
+    has_after, has_before = section < sections - 1, section > 0
+    section_after, section_before = section + 1, section - 1
+
+    barrier = pltpu.get_barrier_semaphore()
+
+    def greet(where):
+        pl.semaphore_signal(barrier, inc=1, device_id=where, device_id_type=MESH)
+
+    for device in (mate, behind, ahead_mate):
+        greet({"expert": device})
+
+    @pl.when(has_before)
+    def _():
+        greet({"section": section_before})
+        greet({"section": section_before, "expert": behind})
 
     loads = [
         pltpu.make_async_copy(source, target, load_sems.at[i])
         for i, (source, target) in enumerate(
             (
+                (in_flight.at[0, role], inflow.at[0, mine]),
+                (norm_gain, gain),
                 (expert_ids, ids),
                 (route_weights, weights),
-                (norm_gain, gain),
-                (in_flight.at[0, role], inflow.at[0, mine]),
                 (arriving.at[0, role], entering.at[mine]),
                 (gate_up.at[0, 0], up_weights),
                 (w_down.at[0, 0], down_weights),
@@ -100,14 +122,17 @@
     for load in loads:
         load.start()
 
-    barrier = pltpu.get_barrier_semaphore()
-    for neighbour in (ahead, behind, mate):
-        pl.semaphore_signal(barrier, inc=1, device_id={"expert": neighbour}, device_id_type=MESH)
-    for neighbour in (section_after, section_before):
-        pl.semaphore_signal(barrier, inc=1, device_id={"section": neighbour}, device_id_type=MESH)
+    def normalize(step, rows, rows_now):
+        wide = inflow[step, rows_now].astype(jnp.float32)
+        inverse = lax.rsqrt(jnp.mean(wide * wide, axis=-1, keepdims=True) + 1e-06)
+        rows[0, rows_now, pl.ds(0, features)] = (wide * inverse * gain[...]).astype(jnp.bfloat16)
 
     loads[0].wait()
     loads[1].wait()
+    normalize(0, rows0, mine)
+
+    loads[2].wait()
+    loads[3].wait()
     line = lax.broadcasted_iota(jnp.int32, (LANES, tokens), 0)
     is_high = lax.rem(line, 2 * experts) < experts
     for micro in range(micros):
@@ -122,8 +147,9 @@
         both = jnp.where(line < 2 * experts, dense[0], dense[1])
         high = both.astype(jnp.bfloat16).astype(jnp.float32)
         shares[micro] = jnp.where(is_high, high, both - high).T.astype(jnp.bfloat16)
-
-    pl.semaphore_wait(barrier, 5)
+    rows0[0, mine, pl.ds(features, LANES)] = shares[role]
+
+    pl.semaphore_wait(barrier, 3 + 2 * has_after.astype(jnp.int32))
 
     def swap(index, source, target):
         return pltpu.make_async_remote_copy(
@@ -131,20 +157,43 @@
         )
 
     swaps = (
-        swap(0, in_flight.at[0, 1 - role], inflow.at[0, mine]),
-        swap(1, shares.at[1 - role], rows0.at[0, mine, pl.ds(features, LANES)]),
-        swap(2, arriving.at[0, 1 - role], entering.at[mine]),
+        swap(0, in_flight.at[0, 1 - role], inflow.at[0, other]),
+        swap(1, shares.at[1 - role], rows0.at[0, other, pl.ds(features, LANES)]),
+        swap(2, arriving.at[0, 1 - role], entering.at[other]),
     )
-    for copy in swaps:
-        copy.start()
-    rows0[0, mine, pl.ds(features, LANES)] = shares[role]
-    sum_in[:, 1] = jnp.zeros((steps,) + sum_in.shape[2:], sum_in.dtype)
+    swaps[0].start()
+    swaps[1].start()
 
     mate_lane = lax.broadcasted_iota(jnp.int32, (2 * group, LANES), 1)
 
+    home_on = pltpu.make_async_remote_copy(
+        home.at[0], home_before, home_send.at[0], home_recv.at[0], {"section": section_after}, MESH
+    )
+    home_over = pltpu.make_async_remote_copy(
+        home.at[1, other], home_mate, home_send.at[1], home_recv.at[1], {"expert": mate}, MESH
+    )
+
+    def sum_to_next_section(i):
+        return pltpu.make_async_remote_copy(
+            sum_out.at[0, chips - 1, chunks[i]],
+            sum_before.at[chunks[i]],
+            before_send,
+            before_recv.at[i],
+            {"section": section_after, "expert": ahead},
+            MESH,
+        )
+
+    def sum_to_owner(i, micro=role):
+        return pltpu.make_async_remote_copy(
+            sum_out.at[1, chips - 1, chunks[i]],
+            sum_last.at[micro, chunks[i % half]],
+            last_send,
+            last_recv.at[micro, i % half],
+            {"expert": ahead if i < half else ahead_mate},
+            MESH,
+        )
+
     def relay_step(step, rows):
-        width = rows.shape[-1]
-
         def pass_on(k, i):
             return pltpu.make_async_remote_copy(
                 rows.at[k, chunks[i]],
@@ -155,10 +204,10 @@
                 MESH,
             )
 
-        def to_mate(k):
+        def to_mate(k, i):
             return pltpu.make_async_remote_copy(
-                rows.at[k, pl.ds(0, group)],
-                rows.at[k, pl.ds(group, group)],
+                rows.at[k, chunks[i]],
+                rows.at[k, pl.ds(group + i * CHUNK, CHUNK)],
                 mate_send.at[step],
                 mate_recv.at[step, k],
                 {"expert": mate},
@@ -192,15 +241,18 @@
             def _():
                 pass_on(k, i).start()
 
+            to_mate(k, i).start()
+
         def multiply_up(k):
-            to_mate(k).wait_recv()
-            block = rows[k, :, pl.ds(0, features)]
+            arrived = rows.at[k, pl.ds(group, group)]
+            pltpu.make_async_copy(arrived, arrived, mate_recv.at[step, k]).wait()
+            both = rows[k, :, pl.ds(0, features)]
             for start in range(0, ff, tile):
                 gate = jnp.dot(
-                    block, up_weights[:, start : start + tile], preferred_element_type=jnp.float32
+                    both, up_weights[:, start : start + tile], preferred_element_type=jnp.float32
                 )
                 lift = jnp.dot(
-                    block,
+                    both,
                     up_weights[:, ff + start : ff + start + tile],
                     preferred_element_type=jnp.float32,
                 )
@@ -234,6 +286,9 @@
             total = own[lax.rem(k, 2), rows_now] + part_in[step, k, rows_now].astype(jnp.float32)
             total = total + sum_in[step, k, rows_now].astype(jnp.float32)
             sum_out[step, k, rows_now] = total.astype(jnp.bfloat16)
+
+        def add_on(k, i):
+            add(k, i)
             sum_on(k, i).start()
 
         def turn(k, carry):
@@ -247,111 +302,138 @@
 
                     @pl.when(k > 2)
                     def _():
-                        add(k - 2, i + 1)
+                        add_on(k - 2, i + 1)
 
                     if i == 0:
                         multiply_up(k - 1)
                     elif i == 1:
                         multiply_down(k - 1)
                 else:
-
-                    @pl.when(k < chips)
+                    part_to_mate(k - 1).wait_recv()
+
+                    @pl.when((k > 1) & (k < chips))
                     def _():
-                        to_mate(k).start()
-
-                    part_to_mate(k - 1).wait_recv()
-
-                    @pl.when(k > 1)
-                    def _():
-                        add(k - 1, 0)
+                        add_on(k - 1, 0)
 
                     @pl.when(k == 1)
                     def _():
-                        home[...] = (
+                        home[step] = (
                             own[0]
                             + part_in[step, 0].astype(jnp.float32)
                             + inflow[step].astype(jnp.float32)
                         )
+                        if step == 0:
+
+                            @pl.when(has_after)
+                            def _():
+                                home_on.start()
+
+                        else:
+                            home_over.start()
 
             return carry
 
         for i, rows_now in enumerate(chunks):
-            prepare(step, rows, rows_now, i)
+            if step == 0 and i == half:
+                swaps[0].wait_recv()
+                swaps[1].wait_recv()
+                normalize(0, rows, other)
+            if step == 1:
+                if i == 0:
+
+                    @pl.when(has_before)
+                    def _():
+                        home_on.wait_recv()
+
+                @pl.when(has_before)
+                def _():
+                    sum_to_next_section(i).wait_recv()
+                    total = home_before[rows_now] + sum_before[rows_now].astype(jnp.float32)
+                    inflow[1, rows_now] = total.astype(jnp.bfloat16)
+
+                @pl.when(section == 0)
+                def _():
+                    inflow[1, rows_now] = entering[rows_now]
+
+                normalize(1, rows, rows_now)
             pass_on(0, i).start()
-        to_mate(0).start()
+            to_mate(0, i).start()
         if step == 0:
+            swaps[2].start()
+            sum_in[:, 1] = jnp.zeros((steps,) + sum_in.shape[2:], sum_in.dtype)
             loads[5].wait()
             loads[6].wait()
         lax.fori_loop(1, chips + 1, turn, 0)
-        for i in range(1, len(chunks)):
+        for i in range(len(chunks)):
             add(chips - 1, i)
-        for i, rows_now in enumerate(chunks):
-            sum_on(chips - 1, i).wait_recv()
-            last = sum_in[step, chips, rows_now].astype(jnp.float32)
-            results[step, rows_now] = (home[rows_now] + last).astype(jnp.bfloat16)
-            if step + 1 < steps:
-                relay(i).start()
-
-    def relay(i):
-        return pltpu.make_async_remote_copy(
-            results.at[0, chunks[i]],
-            shifted.at[chunks[i]],
-            shift_send,
-            shift_recv.at[i],
-            {"section": section_after},
-            MESH,
+            if step == 0:
+
+                @pl.when(has_after)
+                def _():
+                    sum_to_next_section(i).start()
+
+                sum_on(chips - 1, i).start()
+            else:
+                sum_to_owner(i).start()
+        if step == 0:
+            loads[4].wait()
+            swaps[2].wait_recv()
+
+    relay_step(0, rows0)
+
+    def first_out():
+        return (
+            pltpu.make_async_copy(first.at[mine], out.at[0, 0, role], out_sems.at[0]),
+            pltpu.make_async_remote_copy(
+                first.at[other], out.at[0, 0, role], out_send, out_recv, {"expert": mate}, MESH
+            ),
         )
 
-    def prepare(step, rows, rows_now, i):
-        if step > 0:
-            relay(i).wait_recv()
-            inflow[step, rows_now] = jnp.where(section == 0, entering[rows_now], shifted[rows_now])
-        wide = inflow[step, rows_now].astype(jnp.float32)
-        inverse = lax.rsqrt(jnp.mean(wide * wide, axis=-1, keepdims=True) + 1e-06)
-        rows[0, rows_now, pl.ds(0, features)] = (wide * inverse * gain[...]).astype(jnp.bfloat16)
-
-    def hand_out(step):
-        local = pltpu.make_async_copy(
-            results.at[step, mine], out.at[step, 0, role], out_sems.at[step]
+    relay_step(1, rows1)
+
+    for i, rows_now in enumerate(chunks):
+        come_round = sum_in.at[0, chips, rows_now]
+        pltpu.make_async_copy(come_round, come_round, sum_recv.at[0, chips, i]).wait()
+        first[rows_now] = (home[0, rows_now] + come_round[...].astype(jnp.float32)).astype(
+            jnp.bfloat16
         )
-        remote = pltpu.make_async_remote_copy(
-            results.at[step, other],
-            out.at[step, 0, role],
-            out_send.at[step],
-            out_recv.at[step],
-            {"expert": mate},
-            MESH,
-        )
-        return local, remote
-
-    loads[2].wait()
-    loads[3].wait()
-    swaps[0].wait_recv()
-    swaps[1].wait_recv()
-    relay_step(0, rows0)
-    for copy in hand_out(0):
+    for copy in first_out():
         copy.start()
-    loads[4].wait()
-    swaps[2].wait_recv()
-    relay_step(1, rows1)
-    for copy in hand_out(1):
-        copy.start()
+
+    home_over.wait_recv()
+    for i in range(half):
+        sum_to_owner(i).wait_recv()
+        total = home[1, chunks[i]] + sum_last[role, chunks[i]].astype(jnp.float32)
+        last[role, chunks[i]] = total.astype(jnp.bfloat16)
+    for i in range(half):
+        sum_to_owner(i, 1 - role).wait_recv()
+        total = home_mate[chunks[i]] + sum_last[1 - role, chunks[i]].astype(jnp.float32)
+        last[1 - role, chunks[i]] = total.astype(jnp.bfloat16)
+    last_out = pltpu.make_async_copy(last, out.at[1, 0], out_sems.at[1])
+    last_out.start()
+
+    def drain(source, sem):
+        pltpu.make_async_copy(source, source, sem).wait()
 
     for copy in swaps:
         copy.wait_send()
 
-    def drain(source, sem):
-        pltpu.make_async_copy(source, source, sem).wait()
-
-    drain(results.at[0], shift_send)
+    @pl.when(has_after)
+    def _():
+        home_on.wait_send()
+        drain(sum_out.at[0, chips - 1], before_send)
+
+    home_over.wait_send()
+    drain(sum_out.at[1, chips - 1], last_send)
     for step, rows in enumerate((rows0, rows1)):
-        drain(rows.at[pl.ds(0, chips - 1), pl.ds(0, group)], row_send.at[step])
-        drain(rows.at[pl.ds(0, chips), pl.ds(0, group)], mate_send.at[step])
+        drain(rows.at[pl.ds(0, chips - 1), block], row_send.at[step])
+        drain(rows.at[pl.ds(0, chips), block], mate_send.at[step])
         drain(part_out.at[step], part_send.at[step])
-        drain(sum_out.at[step, pl.ds(1, chips - 1)], sum_send.at[step])
-        local, remote = hand_out(step)
-        local.wait()
-        remote.wait()
+        sums = pl.ds(1, chips - 1 - step)
+        drain(sum_out.at[step, sums], sum_send.at[step])
+    for copy in first_out():
+        copy.wait()
+    last_out.wait()
 
 
 def local(in_flight, arriving, norm_gain, gate_up, w_down, expert_ids, route_weights):
@@ -360,6 +442,7 @@
     steps = expert_ids.shape[0]
     ff = w_down.shape[2]
     group = 2 * tokens
+    pieces = group // CHUNK
     expert_ids, route_weights = expert_ids.swapaxes(3, 4), route_weights.swapaxes(3, 4)
     half, full = jnp.bfloat16, jnp.float32
     dma = pltpu.SemaphoreType.DMA
@@ -378,11 +461,15 @@
             pltpu.VMEM((steps, chips) + block, half),
             pltpu.VMEM((steps, chips) + block, half),
             pltpu.VMEM((2,) + block, full),
+            pltpu.VMEM((steps,) + block, full),
             pltpu.VMEM(block, full),
+            pltpu.VMEM((tokens, features), full),
             pltpu.VMEM((steps,) + block, half),
             pltpu.VMEM(block, half),
             pltpu.VMEM(block, half),
-            pltpu.VMEM((steps,) + block, half),
+            pltpu.VMEM((micros, tokens, features), half),
+            pltpu.VMEM(block, half),
+            pltpu.VMEM((micros, tokens, features), half),
             pltpu.VMEM((2 * group, ff), half),
             pltpu.VMEM((micros, tokens, LANES), half),
             pltpu.VMEM((1, features), full),
@@ -394,17 +481,21 @@
             dma((3,)),
             dma((3,)),
             dma((steps,)),
-            dma((steps, chips, group // CHUNK)),
+            dma((steps, chips, pieces)),
             dma((steps,)),
             dma((steps, chips)),
             dma((steps,)),
-            dma((steps, chips + 1, group // CHUNK)),
+            dma((steps, chips + 1, pieces)),
             dma((steps,)),
             dma((steps, chips)),
+            dma((2,)),
+            dma((2,)),
             dma,
-            dma((group // CHUNK,)),
-            dma((steps,)),
-            dma((steps,)),
+            dma((pieces,)),
+            dma,
+            dma((micros, pieces // 2)),
+            dma,
+            dma,
             dma((steps,)),
         ],
         compiler_params=pltpu.CompilerParams(

time: 136 us -> 128 us (0.941)
  the two profiles are of different devices: /device:TPU:1 before, /device:TPU:25 now
where the time goes in v4:
time: 128 us
  Pallas kernels  126 us (98%)
  local copies, waits for them, and re-layouts  1.67 us (1%)
    pallas_call x1, Pallas kernels, local(): pl.pallas_call(functools.partial(relay_kernel, chips, sections), out_shap...  126 us

profile of v4, /device:TPU:25, one launch (start us, length us, event | category | flops | bytes accessed | tf_op | source)
XLA Modules:
  0.0 128.0 jit_solution(10860790492878702764)
XLA Ops:
  0.0 126.3 %relay.1 = bf16[2,1,2,32,1024]{4,3,2,1,0:T(8,128)(2,1)} custom-call(bf16[1,2,32,1024]{3,2,1,0:T(8,128)(2,1)} %in_flight.1, bf16[1,2,32,1024]{3,2,1,0:T(8,128)(2,1)} %arriving.1, f32[1,1024]{1,0:T(1,128)} %norm_gain.1, bf16[1,1,1024,1536]{3,2,1,0:T(8,128)(2,1)} %gate_up.1, bf16[1,1,768,1024]{3,2,1,0:T(8,128)(2,1)} %w_down.1, s32[2,1,2,8,32]{4,3,2,1,0:T(8,128)} %bitcast.2, ...), custom_call_target="tpu_custom_call" | custom-call | tf_op jit(solution)/shard_map/relay/pallas_call | solution.py:451
  126.4 1.7 %copy.9 = bf16[2,1,2,32,1024]{4,3,2,1,0:T(8,128)(2,1)} copy(bf16[2,1,2,32,1024]{4,3,2,1,0:T(8,128)(2,1)} %relay.1) | data formatting | bytes 524288

commit v5 on v4

--- a/solution.py
+++ b/solution.py
@@ -10,6 +10,25 @@
 MESH = pl.DeviceIdType.MESH
 LANES = 128
 CHUNK = 16
+TURN = (
+    ("row", 0, 0),
+    ("sum", 2, 3),
+    ("down", 1, 0),
+    ("row", 0, 1),
+    ("row", 0, 2),
+    ("row", 0, 3),
+    ("part", 1, 0),
+    ("sum", 1, 0),
+    ("sum", 1, 1),
+    ("sum", 1, 2),
+    ("up", 0, 0),
+)
+
+
+def when(condition):
+    if isinstance(condition, bool):
+        return (lambda work: work()) if condition else (lambda work: None)
+    return pl.when(condition)
 
 
 def relay_kernel(
@@ -127,9 +146,19 @@
         inverse = lax.rsqrt(jnp.mean(wide * wide, axis=-1, keepdims=True) + 1e-06)
         rows[0, rows_now, pl.ds(0, features)] = (wide * inverse * gain[...]).astype(jnp.bfloat16)
 
-    loads[0].wait()
-    loads[1].wait()
-    normalize(0, rows0, mine)
+    pl.semaphore_wait(barrier, 3 + 2 * has_after.astype(jnp.int32))
+
+    def swap(index, source, target):
+        return pltpu.make_async_remote_copy(
+            source, target, swap_send.at[index], swap_recv.at[index], {"expert": mate}, MESH
+        )
+
+    swaps = (
+        swap(0, in_flight.at[0, 1 - role], inflow.at[0, other]),
+        swap(1, shares.at[1 - role], rows0.at[0, other, pl.ds(features, LANES)]),
+        swap(2, arriving.at[0, 1 - role], entering.at[other]),
+    )
+    swaps[0].start()
 
     loads[2].wait()
     loads[3].wait()
@@ -147,22 +176,12 @@
         both = jnp.where(line < 2 * experts, dense[0], dense[1])
         high = both.astype(jnp.bfloat16).astype(jnp.float32)
         shares[micro] = jnp.where(is_high, high, both - high).T.astype(jnp.bfloat16)
+    swaps[1].start()
     rows0[0, mine, pl.ds(features, LANES)] = shares[role]
 
-    pl.semaphore_wait(barrier, 3 + 2 * has_after.astype(jnp.int32))
-
-    def swap(index, source, target):
-        return pltpu.make_async_remote_copy(
-            source, target, swap_send.at[index], swap_recv.at[index], {"expert": mate}, MESH
-        )
-
-    swaps = (
-        swap(0, in_flight.at[0, 1 - role], inflow.at[0, other]),
-        swap(1, shares.at[1 - role], rows0.at[0, other, pl.ds(features, LANES)]),
-        swap(2, arriving.at[0, 1 - role], entering.at[other]),
-    )
-    swaps[0].start()
-    swaps[1].start()
+    loads[0].wait()
+    loads[1].wait()
+    normalize(0, rows0, mine)
 
     mate_lane = lax.broadcasted_iota(jnp.int32, (2 * group, LANES), 1)
 
@@ -291,47 +310,54 @@
             add(k, i)
             sum_on(k, i).start()
 
-        def turn(k, carry):
-            for i in range(len(chunks)):
-
-                @pl.when(k < chips)
+        def take_part(k):
+            part_to_mate(k).wait_recv()
+
+            @when(k == 0)
+            def _():
+                home[step] = (
+                    own[0]
+                    + part_in[step, 0].astype(jnp.float32)
+                    + inflow[step].astype(jnp.float32)
+                )
+                if step == 0:
+
+                    @pl.when(has_after)
+                    def _():
+                        home_on.start()
+
+                else:
+                    home_over.start()
+
+        def finish(i):
+            add(chips - 1, i)
+            if step == 0:
+
+                @pl.when(has_after)
                 def _():
-                    forward(k, i)
-
-                if i < len(chunks) - 1:
-
-                    @pl.when(k > 2)
-                    def _():
-                        add_on(k - 2, i + 1)
-
-                    if i == 0:
-                        multiply_up(k - 1)
-                    elif i == 1:
-                        multiply_down(k - 1)
+                    sum_to_next_section(i).start()
+
+            else:
+                sum_to_owner(i).start()
+
+        def turn(k):
+            for what, behind_by, i in TURN:
+                b = k - behind_by
+                if isinstance(b, int) and not 0 <= b < chips:
+                    continue
+                if what == "row":
+                    if not isinstance(b, int) or b > 0:
+                        forward(b, i)
+                elif what == "up":
+                    when(b >= 0)(functools.partial(multiply_up, b))
+                elif what == "down":
+                    when(b >= 0)(functools.partial(multiply_down, b))
+                elif what == "part":
+                    when(b >= 0)(functools.partial(take_part, b))
+                elif isinstance(b, int) and b == chips - 1:
+                    finish(i)
                 else:
-                    part_to_mate(k - 1).wait_recv()
-
-                    @pl.when((k > 1) & (k < chips))
-                    def _():
-                        add_on(k - 1, 0)
-
-                    @pl.when(k == 1)
-                    def _():
-                        home[step] = (
-                            own[0]
-                            + part_in[step, 0].astype(jnp.float32)
-                            + inflow[step].astype(jnp.float32)
-                        )
-                        if step == 0:
-
-                            @pl.when(has_after)
-                            def _():
-                                home_on.start()
-
-                        else:
-                            home_over.start()
-
-            return carry
+                    when(b > 0)(functools.partial(add_on, b, i))
 
         for i, rows_now in enumerate(chunks):
             if step == 0 and i == half:
@@ -363,19 +389,13 @@
             sum_in[:, 1] = jnp.zeros((steps,) + sum_in.shape[2:], sum_in.dtype)
             loads[5].wait()
             loads[6].wait()
-        lax.fori_loop(1, chips + 1, turn, 0)
-        for i in range(len(chunks)):
-            add(chips - 1, i)
-            if step == 0:
-
-                @pl.when(has_after)
-                def _():
-                    sum_to_next_section(i).start()
-
+        turn(0)
+        pl.loop(1, chips)(turn)
+        for k in range(chips, chips + 1 + max(behind_by for _, behind_by, _ in TURN)):
+            turn(k)
+        if step == 0:
+            for i in range(len(chunks)):
                 sum_on(chips - 1, i).start()
-            else:
-                sum_to_owner(i).start()
-        if step == 0:
             loads[4].wait()
             swaps[2].wait_recv()
 
@@ -450,9 +470,9 @@
     anywhere = pl.BlockSpec(memory_space=pl.ANY)
     return pl.pallas_call(
         functools.partial(relay_kernel, chips, sections),
-        out_shape=jax.ShapeDtypeStruct((steps, 1, micros, tokens, features), half),
+        out_shape=pltpu.VMEM((steps, 1, micros, tokens, features), half),
         in_specs=[anywhere] * 7,
-        out_specs=anywhere,
+        out_specs=pl.BlockSpec(memory_space=pltpu.VMEM),
         scratch_shapes=[
             pltpu.VMEM((chips, 2 * group, features + LANES), half),
             pltpu.VMEM((chips, 2 * group, features), half),

time: 128 us -> 126 us (0.984)
  no operation moved by 1% of the time
where the time goes in v5:
time: 126 us
  Pallas kernels  126 us (100%)
    pallas_call x1, Pallas kernels, local(): pl.pallas_call(functools.partial(relay_kernel, chips, sections), out_shap...  126 us

profile of v5, /device:TPU:25, one launch (start us, length us, event | category | flops | bytes accessed | tf_op | source)
XLA Modules:
  0.0 126.3 jit_solution(6325308995233885820)
XLA Ops:
  0.0 125.6 %relay.1 = bf16[2,1,2,32,1024]{4,3,2,1,0:T(8,128)(2,1)S(1)} custom-call(bf16[1,2,32,1024]{3,2,1,0:T(8,128)(2,1)} %in_flight.1, bf16[1,2,32,1024]{3,2,1,0:T(8,128)(2,1)} %arriving.1, f32[1,1024]{1,0:T(1,128)} %norm_gain.1, bf16[1,1,1024,1536]{3,2,1,0:T(8,128)(2,1)} %gate_up.1, bf16[1,1,768,1024]{3,2,1,0:T(8,128)(2,1)} %w_down.1, s32[2,1,2,8,32]{4,3,2,1,0:T(8,128)} %bitcast.2, ...), custom_call_target="tpu_custom_call" | custom-call | tf_op jit(solution)/shard_map/relay/pallas_call | solution.py:471
  125.6 0.7 copy.9

commit v6 on v5

--- a/solution.py
+++ b/solution.py
@@ -42,8 +42,9 @@
     expert_ids,
     route_weights,
     out,
-    rows0,
-    rows1,
+    rows,
+    cards,
+    card_in,
     sum_in,
     sum_out,
     part_out,
@@ -72,6 +73,10 @@
     row_recv,
     mate_send,
     mate_recv,
+    card_send,
+    card_recv,
+    card_mate_send,
+    card_mate_recv,
     sum_send,
     sum_recv,
     part_send,
@@ -141,10 +146,10 @@
     for load in loads:
         load.start()
 
-    def normalize(step, rows, rows_now):
+    def normalize(step, rows_now):
         wide = inflow[step, rows_now].astype(jnp.float32)
         inverse = lax.rsqrt(jnp.mean(wide * wide, axis=-1, keepdims=True) + 1e-06)
-        rows[0, rows_now, pl.ds(0, features)] = (wide * inverse * gain[...]).astype(jnp.bfloat16)
+        rows[step, 0, rows_now] = (wide * inverse * gain[...]).astype(jnp.bfloat16)
 
     pl.semaphore_wait(barrier, 3 + 2 * has_after.astype(jnp.int32))
 
@@ -155,35 +160,17 @@
 
     swaps = (
         swap(0, in_flight.at[0, 1 - role], inflow.at[0, other]),
-        swap(1, shares.at[1 - role], rows0.at[0, other, pl.ds(features, LANES)]),
+        swap(1, shares.at[1 - role], card_in),
         swap(2, arriving.at[0, 1 - role], entering.at[other]),
     )
     swaps[0].start()
 
-    loads[2].wait()
-    loads[3].wait()
-    line = lax.broadcasted_iota(jnp.int32, (LANES, tokens), 0)
-    is_high = lax.rem(line, 2 * experts) < experts
-    for micro in range(micros):
-        dense = []
-        for step in range(steps):
-            step_ids, step_weights = ids[step, 0, micro], weights[step, 0, micro]
-            total = jnp.zeros((LANES, tokens), jnp.float32)
-            for k in range(top_count):
-                named = step_ids[k : k + 1] == lax.rem(line, experts)
-                total = total + jnp.where(named, step_weights[k : k + 1], 0.0)
-            dense.append(total)
-        both = jnp.where(line < 2 * experts, dense[0], dense[1])
-        high = both.astype(jnp.bfloat16).astype(jnp.float32)
-        shares[micro] = jnp.where(is_high, high, both - high).T.astype(jnp.bfloat16)
-    swaps[1].start()
-    rows0[0, mine, pl.ds(features, LANES)] = shares[role]
 
     loads[0].wait()
     loads[1].wait()
-    normalize(0, rows0, mine)
-
-    mate_lane = lax.broadcasted_iota(jnp.int32, (2 * group, LANES), 1)
+    normalize(0, mine)
+
+    card_lane = lax.broadcasted_iota(jnp.int32, (tokens, LANES), 1)
 
     home_on = pltpu.make_async_remote_copy(
         home.at[0], home_before, home_send.at[0], home_recv.at[0], {"section": section_after}, MESH
@@ -212,11 +199,40 @@
             MESH,
         )
 
-    def relay_step(step, rows):
+    def card_on(k):
+        return pltpu.make_async_remote_copy(
+            cards.at[k, mine], cards.at[k + 1, mine], card_send, card_recv.at[k + 1], {"expert": ahead}, MESH
+        )
+
+    def card_to_mate(k):
+        return pltpu.make_async_remote_copy(
+            cards.at[k, mine], cards.at[k, other], card_mate_send, card_mate_recv.at[k], {"expert": mate}, MESH
+        )
+
+    def make_cards():
+        loads[2].wait()
+        loads[3].wait()
+        line = lax.broadcasted_iota(jnp.int32, (LANES, tokens), 0)
+        for micro in range(micros):
+            dense = []
+            for step in range(steps):
+                step_ids, step_weights = ids[step, 0, micro], weights[step, 0, micro]
+                total = jnp.zeros((LANES, tokens), jnp.float32)
+                for k in range(top_count):
+                    named = step_ids[k : k + 1] == lax.rem(line, experts)
+                    total = total + jnp.where(named, step_weights[k : k + 1], 0.0)
+                dense.append(total)
+            both = jnp.where(lax.rem(line, 2 * experts) < experts, dense[0], dense[1])
+            side = line // (2 * experts)
+            both = jnp.where(side == jnp.where(role == micro, 0, 1), both, 0.0)
+            shares[micro] = both.T.astype(jnp.bfloat16)
+        swaps[1].start()
+
+    def relay_step(step):
         def pass_on(k, i):
             return pltpu.make_async_remote_copy(
-                rows.at[k, chunks[i]],
-                rows.at[k + 1, chunks[i]],
+                rows.at[step, k, chunks[i]],
+                rows.at[step, k + 1, chunks[i]],
                 row_send.at[step],
                 row_recv.at[step, k + 1, i],
                 {"expert": ahead},
@@ -225,8 +241,8 @@
 
         def to_mate(k, i):
             return pltpu.make_async_remote_copy(
-                rows.at[k, chunks[i]],
-                rows.at[k, pl.ds(group + i * CHUNK, CHUNK)],
+                rows.at[step, k, chunks[i]],
+                rows.at[step, k, pl.ds(group + i * CHUNK, CHUNK)],
                 mate_send.at[step],
                 mate_recv.at[step, k],
                 {"expert": mate},
@@ -261,11 +277,19 @@
                 pass_on(k, i).start()
 
             to_mate(k, i).start()
+            if step == 0 and i == len(chunks) - 1:
+                card_on(k - 1).wait_recv()
+
+                @pl.when(k < chips - 1)
+                def _():
+                    card_on(k).start()
+
+                card_to_mate(k).start()
 
         def multiply_up(k):
-            arrived = rows.at[k, pl.ds(group, group)]
+            arrived = rows.at[step, k, pl.ds(group, group)]
             pltpu.make_async_copy(arrived, arrived, mate_recv.at[step, k]).wait()
-            both = rows[k, :, pl.ds(0, features)]
+            both = rows[step, k]
             for start in range(0, ff, tile):
                 gate = jnp.dot(
                     both, up_weights[:, start : start + tile], preferred_element_type=jnp.float32
@@ -281,10 +305,16 @@
 
         def multiply_down(k):
             slot = lax.rem(k, 2)
-            at = step * 2 * experts + me
-            picked = (mate_lane == at) | (mate_lane == at + experts)
-            share = rows0[k, :, pl.ds(features, LANES)].astype(jnp.float32)
-            share = jnp.sum(jnp.where(picked, share, 0.0), axis=1, keepdims=True)
+            if step == 0:
+                card_to_mate(k).wait_recv()
+            at = step * experts + me
+            share = []
+            for card_rows in (mine, other):
+                card = cards[k, card_rows].astype(jnp.float32)
+                for lane in (at, at + 2 * experts):
+                    picked = jnp.where(card_lane == lane, card, 0.0)
+                    share.append(jnp.sum(picked, axis=1, keepdims=True))
+            share = jnp.concatenate(share, axis=0)
             for start in range(0, features, tile):
                 result = jnp.dot(
                     hidden[...],
@@ -361,9 +391,9 @@
 
         for i, rows_now in enumerate(chunks):
             if step == 0 and i == half:
+                make_cards()
                 swaps[0].wait_recv()
-                swaps[1].wait_recv()
-                normalize(0, rows, other)
+                normalize(0, other)
             if step == 1:
                 if i == 0:
 
@@ -381,10 +411,14 @@
                 def _():
                     inflow[1, rows_now] = entering[rows_now]
 
-                normalize(1, rows, rows_now)
+                normalize(1, rows_now)
             pass_on(0, i).start()
             to_mate(0, i).start()
         if step == 0:
+            swaps[1].wait_recv()
+            cards[0, mine] = shares[role] + card_in[...]
+            card_on(0).start()
+            card_to_mate(0).start()
             swaps[2].start()
             sum_in[:, 1] = jnp.zeros((steps,) + sum_in.shape[2:], sum_in.dtype)
             loads[5].wait()
@@ -399,7 +433,7 @@
             loads[4].wait()
             swaps[2].wait_recv()
 
-    relay_step(0, rows0)
+    relay_step(0)
 
     def first_out():
         return (
@@ -409,7 +443,7 @@
             ),
         )
 
-    relay_step(1, rows1)
+    relay_step(1)
 
     for i, rows_now in enumerate(chunks):
         come_round = sum_in.at[0, chips, rows_now]
@@ -445,9 +479,11 @@
 
     home_over.wait_send()
     drain(sum_out.at[1, chips - 1], last_send)
-    for step, rows in enumerate((rows0, rows1)):
-        drain(rows.at[pl.ds(0, chips - 1), block], row_send.at[step])
-        drain(rows.at[pl.ds(0, chips), block], mate_send.at[step])
+    drain(cards.at[pl.ds(0, chips - 1), mine], card_send)
+    drain(cards.at[pl.ds(0, chips), mine], card_mate_send)
+    for step in range(steps):
+        drain(rows.at[step, pl.ds(0, chips - 1), block], row_send.at[step])
+        drain(rows.at[step, pl.ds(0, chips), block], mate_send.at[step])
         drain(part_out.at[step], part_send.at[step])
         sums = pl.ds(1, chips - 1 - step)
         drain(sum_out.at[step, sums], sum_send.at[step])
@@ -474,8 +510,9 @@
         in_specs=[anywhere] * 7,
         out_specs=pl.BlockSpec(memory_space=pltpu.VMEM),
         scratch_shapes=[
-            pltpu.VMEM((chips, 2 * group, features + LANES), half),
-            pltpu.VMEM((chips, 2 * group, features), half),
+            pltpu.VMEM((steps, chips, 2 * group, features), half),
+            pltpu.VMEM((chips, group, LANES), half),
+            pltpu.VMEM((tokens, LANES), half),
             pltpu.VMEM((steps, chips + 1) + block, half),
             pltpu.VMEM((steps, chips) + block, half),
             pltpu.VMEM((steps, chips) + block, half),
@@ -504,6 +541,10 @@
             dma((steps, chips, pieces)),
             dma((steps,)),
             dma((steps, chips)),
+            dma,
+            dma((chips,)),
+            dma,
+            dma((chips,)),
             dma((steps,)),
             dma((steps, chips + 1, pieces)),
             dma((steps,)),

time: 126 us -> 126 us (level)
  no operation moved by 1% of the time
where the time goes in v6:
time: 126 us
  Pallas kernels  125 us (99%)
    pallas_call x1, Pallas kernels, local(): pl.pallas_call(functools.partial(relay_kernel, chips, sections), out_shap...  125 us

profile of v6, /device:TPU:25, one launch (start us, length us, event | category | flops | bytes accessed | tf_op | source)
XLA Modules:
  0.0 125.6 jit_solution(5960380541440053042)
XLA Ops:
  0.0 124.9 %relay.1 = bf16[2,1,2,32,1024]{4,3,2,1,0:T(8,128)(2,1)S(1)} custom-call(bf16[1,2,32,1024]{3,2,1,0:T(8,128)(2,1)} %in_flight.1, bf16[1,2,32,1024]{3,2,1,0:T(8,128)(2,1)} %arriving.1, f32[1,1024]{1,0:T(1,128)} %norm_gain.1, bf16[1,1,1024,1536]{3,2,1,0:T(8,128)(2,1)} %gate_up.1, bf16[1,1,768,1024]{3,2,1,0:T(8,128)(2,1)} %w_down.1, s32[2,1,2,8,32]{4,3,2,1,0:T(8,128)} %bitcast.2, ...), custom_call_target="tpu_custom_call" | custom-call | tf_op jit(solution)/shard_map/relay/pallas_call | solution.py:507
  124.9 0.7 copy.9

commit v7 on v6

--- a/solution.py
+++ b/solution.py
@@ -228,6 +228,16 @@
             shares[micro] = both.T.astype(jnp.bfloat16)
         swaps[1].start()
 
+    def come_home():
+        return pltpu.make_async_remote_copy(
+            sum_out.at[0, chips - 1],
+            sum_in.at[0, chips],
+            sum_send.at[0],
+            sum_recv.at[0, chips, 0],
+            {"expert": ahead},
+            MESH,
+        )
+
     def relay_step(step):
         def pass_on(k, i):
             return pltpu.make_async_remote_copy(
@@ -290,16 +300,16 @@
             arrived = rows.at[step, k, pl.ds(group, group)]
             pltpu.make_async_copy(arrived, arrived, mate_recv.at[step, k]).wait()
             both = rows[step, k]
-            for start in range(0, ff, tile):
+            for start in range(0, ff, ff):
                 gate = jnp.dot(
-                    both, up_weights[:, start : start + tile], preferred_element_type=jnp.float32
+                    both, up_weights[:, start : start + ff], preferred_element_type=jnp.float32
                 )
                 lift = jnp.dot(
                     both,
-                    up_weights[:, ff + start : ff + start + tile],
+                    up_weights[:, ff + start : ff + start + ff],
                     preferred_element_type=jnp.float32,
                 )
-                hidden[:, start : start + tile] = (gate / (1.0 + jnp.exp(-gate)) * lift).astype(
+                hidden[:, start : start + ff] = (gate / (1.0 + jnp.exp(-gate)) * lift).astype(
                     jnp.bfloat16
                 )
 
@@ -414,6 +424,8 @@
                 normalize(1, rows_now)
             pass_on(0, i).start()
             to_mate(0, i).start()
+        if step == 1:
+            come_home().start()
         if step == 0:
             swaps[1].wait_recv()
             cards[0, mine] = shares[role] + card_in[...]
@@ -428,8 +440,6 @@
         for k in range(chips, chips + 1 + max(behind_by for _, behind_by, _ in TURN)):
             turn(k)
         if step == 0:
-            for i in range(len(chunks)):
-                sum_on(chips - 1, i).start()
             loads[4].wait()
             swaps[2].wait_recv()
 
@@ -445,9 +455,9 @@
 
     relay_step(1)
 
-    for i, rows_now in enumerate(chunks):
+    come_home().wait_recv()
+    for rows_now in chunks:
         come_round = sum_in.at[0, chips, rows_now]
-        pltpu.make_async_copy(come_round, come_round, sum_recv.at[0, chips, i]).wait()
         first[rows_now] = (home[0, rows_now] + come_round[...].astype(jnp.float32)).astype(
             jnp.bfloat16
         )

time: 126 us -> 125 us (level)
  no operation moved by 1% of the time
where the time goes in v7:
time: 125 us
  Pallas kernels  125 us (100%)
    pallas_call x1, Pallas kernels, local(): pl.pallas_call(functools.partial(relay_kernel, chips, sections), out_shap...  125 us

profile of v7, /device:TPU:25, one launch (start us, length us, event | category | flops | bytes accessed | tf_op | source)
XLA Modules:
  0.0 125.2 jit_solution(9702655190766134811)
XLA Ops:
  0.0 124.5 %relay.1 = bf16[2,1,2,32,1024]{4,3,2,1,0:T(8,128)(2,1)S(1)} custom-call(bf16[1,2,32,1024]{3,2,1,0:T(8,128)(2,1)} %in_flight.1, bf16[1,2,32,1024]{3,2,1,0:T(8,128)(2,1)} %arriving.1, f32[1,1024]{1,0:T(1,128)} %norm_gain.1, bf16[1,1,1024,1536]{3,2,1,0:T(8,128)(2,1)} %gate_up.1, bf16[1,1,768,1024]{3,2,1,0:T(8,128)(2,1)} %w_down.1, s32[2,1,2,8,32]{4,3,2,1,0:T(8,128)} %bitcast.2, ...), custom_call_target="tpu_custom_call" | custom-call | tf_op jit(solution)/shard_map/relay/pallas_call | solution.py:517
  124.5 0.7 copy.9
